TPU v7x, 32 devices: a whole 2x2x4 slice. The times are simulated.
32 devices in a mesh: section: 4 (over x, core), lon: 4 (over z), lat: 2 (over y).
Axes of the slice: x: 2, y: 2, z: 4, core: 2. Of those that a mesh axis runs over, the one named last changes fastest.
Arguments:
- inputs: bfloat16 [4, 8, 12, 48, 192], P('section', None, 'lat', 'lon'), may hold values from -6 to 6
- grad_output: bfloat16 [4, 8, 12, 48, 192], P('section', None, 'lat', 'lon'), may hold values from -6 to 6
- norm_gains: float32 [4, 2, 2, 192], P('section'), may hold values from 0.25 to 1.75
- input_weight: bfloat16 [4, 2, 192, 576], P('section'), may hold values from -0.4375 to 0.4375
- output_weight: bfloat16 [4, 2, 192, 192], P('section'), may hold values from -0.4375 to 0.4375
- expand_weight: bfloat16 [4, 2, 192, 768], P('section'), may hold values from -0.4375 to 0.4375
- reduce_weight: bfloat16 [4, 2, 768, 192], P('section'), may hold values from -0.21875 to 0.21875
- bias_table: float32 [4, 2, 4, 2, 6, 3312], P('section'), may hold values from -4 to 400
Outputs:
- upstream: bfloat16 [4, 8, 12, 48, 192], P('section', None, 'lat', 'lon')
- input_weight_grad: float32 [4, 2, 192, 576], P('section')
- output_weight_grad: float32 [4, 2, 192, 192], P('section')
- expand_weight_grad: float32 [4, 2, 192, 768], P('section')
- reduce_weight_grad: float32 [4, 2, 768, 192], P('section')
- norm_gain_grad: float32 [4, 2, 2, 192], P('section')
- bias_table_grad: float32 [4, 2, 4, 2, 6, 3312], P('section')
All inputs are finite; a program needn't handle non-finite values.
Results may differ from a plain program's by a relative error of at most 0.04.
Values may be sent and summed in bfloat16 or wider, within the bound.
A program may use at most 128 MiB of HBM per device.

v0:
```python
import jax
import jax.numpy as jnp
from jax import lax
from jax.sharding import PartitionSpec as P

MODEL_WIDTH = 192
HEADS = 6
HEAD_SIZE = 32
LEVELS = 8
WIN_LEVELS = 2
WIN_LAT = 6
WIN_LON = 12
BLOCKS = 2
LAT_DEV = 6
LON_DEV = 12
WIN_TOKENS = 144
BIAS_SLOTS = 3312


NORM_EPS = 1e-05
MASK_FILL = -10000.0


def swapped(value, axis, stride):
    mask = 2**stride
    pairs = [(source, source ^ mask) for source in range(lax.axis_size(axis))]
    return lax.ppermute(value, axis, pairs)


def from_behind(x, axis, by):
    size = lax.axis_size(axis)
    return lax.ppermute(x, axis, [(i, (i + by) % size) for i in range(size)])


def from_behind_2(x, axis, by):
    size = lax.axis_size(axis)
    pairs = [(i, i + by) for i in range(size) if 0 <= i + by < size]
    return lax.ppermute(x, axis, pairs)


def layer_norm(activity, gain_vec):
    centred = activity - jnp.mean(activity, axis=-1, keepdims=True)
    spread = jnp.mean(centred * centred, axis=-1, keepdims=True)
    return centred * lax.rsqrt(spread + NORM_EPS) * gain_vec


def gelu_tanh(activity):
    return jax.nn.gelu(activity, approximate=True)


def to_windows(tokens_in):
    levels_n, rows_n, cols_n, chans = tokens_in.shape
    shaped = tokens_in.reshape(
        levels_n // WIN_LEVELS,
        WIN_LEVELS,
        rows_n // WIN_LAT,
        WIN_LAT,
        cols_n // WIN_LON,
        WIN_LON,
        chans,
    )
    shaped = shaped.transpose(0, 2, 4, 1, 3, 5, 6)
    return shaped.reshape(
        levels_n // WIN_LEVELS, rows_n // WIN_LAT, cols_n // WIN_LON, WIN_TOKENS, chans
    )


def from_windows(blocks_in):
    level_w, lat_w, lon_w, _, chans = blocks_in.shape
    shaped = blocks_in.reshape(level_w, lat_w, lon_w, WIN_LEVELS, WIN_LAT, WIN_LON, chans)
    shaped = shaped.transpose(0, 3, 1, 4, 2, 5, 6)
    return shaped.reshape(level_w * WIN_LEVELS, lat_w * WIN_LAT, lon_w * WIN_LON, chans)


def pair_map():
    offsets = 2 * WIN_LON - 1
    group_count = WIN_LEVELS * WIN_LAT
    inner = jnp.arange(group_count * offsets, dtype=jnp.int32)
    inner_group = inner // offsets
    inner_off = inner % offsets
    keys_all = jnp.arange(WIN_TOKENS, dtype=jnp.int32)
    key_group = keys_all // WIN_LON
    key_col = keys_all % WIN_LON
    query_col = jnp.arange(WIN_LON, dtype=jnp.int32)
    same_group = inner_group[:, None, None] == key_group[None, None, :]
    same_off = (
        inner_off[:, None, None] == query_col[None, :, None] - key_col[None, None, :] + WIN_LON - 1
    )
    table = jnp.logical_and(same_group, same_off).astype(jnp.float32)
    return table.reshape(group_count * offsets, WIN_LON * WIN_TOKENS)


def region(position, extent, window_len):
    return jnp.where(
        position < extent - window_len, 0, jnp.where(position < extent - window_len // 2, 1, 2)
    ).astype(jnp.int32)


def dense_bias(table_rows, spread_map, first_row, lat_total, shifted):
    leading = table_rows.shape[:-1]
    group_count = WIN_LEVELS * WIN_LAT
    rows = table_rows.reshape(
        leading + (WIN_LEVELS, WIN_LEVELS, WIN_LAT, WIN_LAT * (2 * WIN_LON - 1))
    )
    rows = jnp.swapaxes(rows, -3, -2)
    rows = rows.reshape(leading + (group_count, group_count * (2 * WIN_LON - 1)))
    spread = jnp.einsum("...rg,gm->...rm", rows, spread_map, precision=lax.Precision.HIGHEST)
    bias_dense = spread.reshape(leading + (WIN_TOKENS, WIN_TOKENS))
    if shifted:
        local_rows = table_rows.shape[1] * WIN_LAT
        level_ids = region(jnp.arange(LEVELS, dtype=jnp.int32), LEVELS, WIN_LEVELS)
        row_ids = region(first_row + jnp.arange(local_rows, dtype=jnp.int32), lat_total, WIN_LAT)
        region_ids = level_ids[:, None] * 3 + row_ids[None, :]
        region_grid = jnp.broadcast_to(
            region_ids[:, :, None, None], (LEVELS, local_rows, WIN_LON, 1)
        )
        token_ids = to_windows(region_grid)[:, :, 0, :, 0]
        matched = token_ids[..., :, None] == token_ids[..., None, :]
        bias_dense = bias_dense + jnp.where(matched, 0.0, MASK_FILL).astype(jnp.float32)[:, :, None]
    return bias_dense[:, :, None]


def mix_tokens(tokens_in, weight):
    token_rows = tokens_in.reshape(-1, tokens_in.shape[-1])
    result = jnp.dot(token_rows, weight, preferred_element_type=jnp.float32)
    return result.reshape(tokens_in.shape[:-1] + (weight.shape[1],))


def mix_back(tokens_in, weight):
    token_rows = tokens_in.reshape(-1, tokens_in.shape[-1])
    result = lax.dot_general(
        token_rows, weight, (((1,), (1,)), ((), ())), preferred_element_type=jnp.float32
    )
    return result.reshape(tokens_in.shape[:-1] + (weight.shape[0],))


def grad_weight(tokens_in, grad_in):
    token_rows = tokens_in.reshape(-1, tokens_in.shape[-1])
    grad_rows = grad_in.reshape(-1, grad_in.shape[-1])
    return lax.dot_general(
        token_rows, grad_rows, (((0,), (0,)), ((), ())), preferred_element_type=jnp.float32
    )


def table_grad(grad_scores, spread_map):
    summed = jnp.sum(grad_scores, axis=2)
    leading = summed.shape[:3]
    group_count = WIN_LEVELS * WIN_LAT
    shaped = summed.reshape(leading + (group_count, WIN_LON * WIN_TOKENS))
    folded = jnp.einsum("...rm,gm->...rg", shaped, spread_map, precision=lax.Precision.HIGHEST)
    folded = folded.reshape(
        leading + (WIN_LEVELS, WIN_LAT, WIN_LEVELS, WIN_LAT * (2 * WIN_LON - 1))
    )
    folded = jnp.swapaxes(folded, -3, -2)
    return folded.reshape(leading + (BIAS_SLOTS,))


def token_major(head_major):
    leading = head_major.shape[:-3]
    merged = head_major.reshape(
        leading + (head_major.shape[-3] * head_major.shape[-2], head_major.shape[-1])
    )
    return jnp.swapaxes(merged, -1, -2)


def attend_forward(windows, bias_dense, input_weight, output_weight):
    leading = windows.shape[:-2]
    token_rows = windows.reshape(-1, MODEL_WIDTH)
    projected = jnp.dot(token_rows, input_weight, preferred_element_type=jnp.float32)
    column_scale = jnp.where(
        jnp.arange(3 * MODEL_WIDTH) < MODEL_WIDTH, HEAD_SIZE ** (-0.5), 1.0
    ).astype(jnp.float32)
    projected_b = (projected * column_scale).astype(jnp.bfloat16)
    heads_all = jnp.swapaxes(projected_b.reshape(leading + (WIN_TOKENS, 3 * MODEL_WIDTH)), -1, -2)
    heads_all = heads_all.reshape(leading + (3, HEADS, HEAD_SIZE, WIN_TOKENS))
    queries = heads_all[..., 0, :, :, :]
    key_part = heads_all[..., 1, :, :, :]
    values = heads_all[..., 2, :, :, :]
    scores = (
        jnp.einsum("...heq,...hek->...hqk", queries, key_part, preferred_element_type=jnp.float32)
        + bias_dense
    )
    attention = jax.nn.softmax(scores, axis=-1)
    weights = attention.astype(jnp.bfloat16)
    mixture_heads = jnp.einsum(
        "...hqk,...hek->...heq", weights, values, preferred_element_type=jnp.float32
    ).astype(jnp.bfloat16)
    mixture = token_major(mixture_heads)
    attended = jnp.dot(
        mixture.reshape(-1, MODEL_WIDTH), output_weight, preferred_element_type=jnp.float32
    )
    return (
        attended.reshape(windows.shape),
        (token_rows, queries, key_part, values, attention, weights, mixture),
    )


def attend_backward(saved, grad_windows_in, input_weight, output_weight):
    token_rows, queries, key_part, values, attention, weights, mixture = saved
    leading = grad_windows_in.shape[:-2]
    grad_rows = grad_windows_in.reshape(-1, MODEL_WIDTH)
    output_grad = grad_weight(mixture.reshape(-1, MODEL_WIDTH), grad_rows)
    grad_mixture = (
        mix_back(grad_rows, output_weight)
        .astype(jnp.bfloat16)
        .reshape(leading + (WIN_TOKENS, MODEL_WIDTH))
    )
    grad_mixture = jnp.swapaxes(grad_mixture, -1, -2).reshape(
        leading + (HEADS, HEAD_SIZE, WIN_TOKENS)
    )
    grad_values = jnp.einsum(
        "...hqk,...heq->...hek", weights, grad_mixture, preferred_element_type=jnp.float32
    )
    grad_weights = jnp.einsum(
        "...heq,...hek->...hqk", grad_mixture, values, preferred_element_type=jnp.float32
    )
    grad_scores = attention * (
        grad_weights - jnp.sum(attention * grad_weights, axis=-1, keepdims=True)
    )
    score_part = grad_scores.astype(jnp.bfloat16)
    grad_queries = jnp.einsum(
        "...hqk,...hek->...heq", score_part, key_part, preferred_element_type=jnp.float32
    ) * HEAD_SIZE ** (-0.5)
    grad_keys = jnp.einsum(
        "...hqk,...heq->...hek", score_part, queries, preferred_element_type=jnp.float32
    )
    grad_heads = jnp.stack([grad_queries, grad_keys, grad_values], axis=-4).astype(jnp.bfloat16)
    grad_projected = token_major(
        grad_heads.reshape(leading + (3 * HEADS, HEAD_SIZE, WIN_TOKENS))
    ).reshape(-1, 3 * MODEL_WIDTH)
    input_grad = grad_weight(token_rows, grad_projected)
    grad_windows = mix_back(grad_projected, input_weight).reshape(grad_windows_in.shape)
    return (grad_windows, input_grad, output_grad, grad_scores)


def lat_trade(edge_rows):
    return swapped(edge_rows, "lat", 0)


def roll_fore(tokens_in):
    half_rows = WIN_LAT // 2
    half_cols = WIN_LON // 2
    moved = jnp.roll(tokens_in, -(WIN_LEVELS // 2), axis=0)
    incoming = lat_trade(moved[:, :half_rows])
    moved = jnp.concatenate([moved[:, half_rows:], incoming], axis=1)
    incoming = from_behind(moved[:, :, :half_cols], "lon", -1)
    return jnp.concatenate([moved[:, :, half_cols:], incoming], axis=2)


def roll_back(tokens_in):
    half_rows = WIN_LAT // 2
    half_cols = WIN_LON // 2
    moved = jnp.roll(tokens_in, WIN_LEVELS // 2, axis=0)
    incoming = from_behind(moved[:, :, -half_cols:], "lon", 1)
    moved = jnp.concatenate([incoming, moved[:, :, :-half_cols]], axis=2)
    incoming = lat_trade(moved[:, -half_rows:])
    return jnp.concatenate([incoming, moved[:, :-half_rows]], axis=1)


def block_forward(
    block_in,
    gain_pair,
    input_weight,
    output_weight,
    expand_weight,
    reduce_weight,
    bias_dense,
    shifted,
):
    block_f = block_in.astype(jnp.float32)
    normed, norm_back = jax.vjp(layer_norm, block_f, gain_pair[0])
    normed_b = normed.astype(jnp.bfloat16)
    framed = roll_fore(normed_b) if shifted else normed_b
    attended, attn_saved = attend_forward(
        to_windows(framed), bias_dense, input_weight, output_weight
    )
    attended = from_windows(attended)
    if shifted:
        attended = roll_back(attended.astype(jnp.bfloat16)).astype(jnp.float32)
    middle = (block_f + attended).astype(jnp.bfloat16)
    middle_f = middle.astype(jnp.float32)
    normed_mid, mid_back = jax.vjp(layer_norm, middle_f, gain_pair[1])
    normed_mid_b = normed_mid.astype(jnp.bfloat16)
    hidden, gelu_back = jax.vjp(gelu_tanh, mix_tokens(normed_mid_b, expand_weight))
    hidden_b = hidden.astype(jnp.bfloat16)
    output = (middle_f + mix_tokens(hidden_b, reduce_weight)).astype(jnp.bfloat16)
    return (output, (norm_back, attn_saved, mid_back, normed_mid_b, gelu_back, hidden_b))


def block_backward(
    saved, grad_in, input_weight, output_weight, expand_weight, reduce_weight, spread_map, shifted
):
    norm_back, attn_saved, mid_back, normed_mid_b, gelu_back, hidden_b = saved
    reduce_grad = grad_weight(hidden_b, grad_in)
    grad_pre = gelu_back(mix_back(grad_in, reduce_weight))[0].astype(jnp.bfloat16)
    expand_grad = grad_weight(normed_mid_b, grad_pre)
    grad_mid_norm, gain_mid_grad = mid_back(mix_back(grad_pre, expand_weight))
    grad_middle = grad_in.astype(jnp.float32) + grad_mid_norm
    grad_middle_b = grad_middle.astype(jnp.bfloat16)
    grad_attended = roll_fore(grad_middle_b) if shifted else grad_middle_b
    grad_windows, input_grad, output_grad, grad_scores = attend_backward(
        attn_saved, to_windows(grad_attended), input_weight, output_weight
    )
    grad_normed = from_windows(grad_windows).astype(jnp.bfloat16)
    if shifted:
        grad_normed = roll_back(grad_normed)
    grad_in_norm, gain_in_grad = norm_back(grad_normed.astype(jnp.float32))
    grad_out = (grad_middle + grad_in_norm).astype(jnp.bfloat16)
    return (
        grad_out,
        (
            input_grad,
            output_grad,
            expand_grad,
            reduce_grad,
            jnp.stack([gain_in_grad, gain_mid_grad]),
            table_grad(grad_scores, spread_map),
        ),
    )


def on_device(
    inputs,
    grad_output,
    norm_gains,
    input_weight,
    output_weight,
    expand_weight,
    reduce_weight,
    bias_table,
):
    lat_index = lax.axis_index("lat")
    window_rows = LAT_DEV // WIN_LAT
    lat_total = LAT_DEV * lax.axis_size("lat")
    first_row = lat_index * LAT_DEV
    first_window = lat_index * window_rows
    spread_map = pair_map()
    savings = []
    block_in = inputs[0]
    for block in range(BLOCKS):
        table_rows = lax.dynamic_slice_in_dim(
            bias_table[0, block], first_window, window_rows, axis=1
        )
        bias_dense = dense_bias(table_rows, spread_map, first_row, lat_total, block % 2 == 1)
        block_in, saved = block_forward(
            block_in,
            norm_gains[0, block],
            input_weight[0, block],
            output_weight[0, block],
            expand_weight[0, block],
            reduce_weight[0, block],
            bias_dense,
            block % 2 == 1,
        )
        savings.append(saved)
    grad_flow = grad_output[0]
    collected = [None] * BLOCKS
    for block in reversed(range(BLOCKS)):
        grad_flow, collected[block] = block_backward(
            savings[block],
            grad_flow,
            input_weight[0, block],
            output_weight[0, block],
            expand_weight[0, block],
            reduce_weight[0, block],
            spread_map,
            block % 2 == 1,
        )
    stacked = [
        jnp.stack([collected[block][index] for block in range(BLOCKS)]) for index in range(6)
    ]
    full_table = lax.dynamic_update_slice_in_dim(
        jnp.zeros(bias_table.shape[1:], jnp.float32), stacked[5], first_window, axis=2
    )
    summed = lax.psum(
        (stacked[0], stacked[1], stacked[2], stacked[3], stacked[4], full_table), ("lon", "lat")
    )
    weight_sums = summed[:5]
    table_out = summed[5]
    grad_scale = float(LEVELS * lat_total * LON_DEV * lax.axis_size("lon")) ** (-0.5)
    upstream = from_behind_2(grad_flow, "section", -1)
    return (
        upstream[None],
        (weight_sums[0] * grad_scale)[None],
        (weight_sums[1] * grad_scale)[None],
        (weight_sums[2] * grad_scale)[None],
        (weight_sums[3] * grad_scale)[None],
        (weight_sums[4] * grad_scale)[None],
        table_out[None],
    )


def solution(mesh):
    return jax.shard_map(
        on_device,
        mesh=mesh,
        in_specs=(
            P("section", None, "lat", "lon", None),
            P("section", None, "lat", "lon", None),
            P("section", None, None, None),
            P("section", None, None, None),
            P("section", None, None, None),
            P("section", None, None, None),
            P("section", None, None, None),
            P("section", None, None, None, None, None),
        ),
        out_specs=(
            P("section", None, "lat", "lon", None),
            P("section", None, None, None),
            P("section", None, None, None),
            P("section", None, None, None),
            P("section", None, None, None),
            P("section", None, None, None),
            P("section", None, None, None, None, None),
        ),
        check_vma=False,
    )
```

profile of v0, /device:TPU:0, one launch (start us, length us, event | category | flops | bytes accessed | tf_op | source)
XLA Modules:
  0.0 423.4 jit_solution(11175264299298419012)
XLA Ops:
  17.5 3.8 copy.88
  26.1 3.9 fusion.156
  29.9 3.5 broadcast_in_dim_reshape.3
  33.4 3.8 copy.91
  40.2 3.4 fusion.152
  60.7 3.6 fusion.157
  68.0 3.6 collective-permute-start.1
  75.7 5.6 %copy.102 = f32[4,6,144,144]{2,3,1,0:T(8,128)} copy(f32[4,6,144,144]{3,2,1,0:T(8,128)} %reshape.859) | data formatting | bytes 3981312 | tf_op jit(solution)/shard_map/reshape | solution.py:108
  90.1 4.2 convolution_convert_fusion.7
  95.4 7.9 %collective-permute-done.2 = bf16[8,6,6,192]{3,2,1,0:T(8,128)(2,1)S(1)} collective-permute-done((bf16[8,6,6,192]{3,2,1,0:T(8,128)(2,1)S(1)}, bf16[8,6,6,192]{3,2,1,0:T(8,128)(2,1)S(1)}, u32[]{:S(2)}, u32[]{:S(2)}) %collective-permute-start.2) | collective-permute-done | bytes 110624 | tf_op jit(solution)/shard_map/ppermute | solution.py:32
  104.1 3.8 reshape.888
  122.8 4.4 %collective-permute-done.5 = bf16[8,6,6,192]{3,2,1,0:T(8,128)(2,1)S(1)} collective-permute-done((bf16[8,6,6,192]{3,2,1,0:T(8,128)(2,1)S(1)}, bf16[8,6,6,192]{3,2,1,0:T(8,128)(2,1)S(1)}, u32[]{:S(2)}, u32[]{:S(2)}) %collective-permute-start.5) | collective-permute-done | bytes 110624 | tf_op jit(solution)/shard_map/ppermute | solution.py:32
  128.9 5.0 %fusion.40 = bf16[4,1,1,1,6,32,144]{6,5,4,0,3,2,1:T(8,128)(2,1)} fusion(bf16[4,6,32,144]{3,2,1,0:T(8,128)(2,1)} %bitcast.382, f32[4,6,144]{2,1,0:T(8,128)} %copy-done.95, f32[4,6,144,144]{2,3,1,0:T(8,128)} %copy-done.4), kind=kOutput, calls=%fused_computation.70 | convolution fusion | flops 33457680 | bytes 2446848 | tf_op jit(solution)/shard_map/...hqk,...heq->...hek/dot_general | solution.py:211
  140.0 3.6 copy.124
  151.9 3.5 reshape.889
  155.4 5.9 %fusion.27 = f32[4,1,6,2,2,6,138]{6,5,4,3,2,0,1:T(8,128)S(1)} fusion(pred[2,138,1728,1,1,1]{2,1,0,3,4,5:T(8,128)(4,1)} %reshape.888, f32[4,6,2,6,1728,1]{4,3,2,1,0,5:T(8,128)} %reshape.889), kind=kOutput, calls=%fused_computation.42 | convolution fusion | flops 1648263168 | bytes 2785536 | tf_op jit(solution)/shard_map/...rm,gm->...rg/dot_general | solution.py:150
  164.2 6.2 %collective-permute-done.6 = bf16[8,6,6,192]{3,2,1,0:T(8,128)(2,1)S(1)} collective-permute-done((bf16[8,6,6,192]{3,2,1,0:T(8,128)(2,1)S(1)}, bf16[8,6,6,192]{3,2,1,0:T(8,128)(2,1)S(1)}, u32[]{:S(2)}, u32[]{:S(2)}) %collective-permute-start.6) | collective-permute-done | bytes 110624 | tf_op jit(solution)/shard_map/ppermute | solution.py:32
  172.2 4.2 collective-permute-done.7
  188.7 5.0 %fusion.42 = bf16[4,1,1,1,6,32,144]{6,5,4,0,3,2,1:T(8,128)(2,1)} fusion(bf16[4,6,32,144]{3,2,1,0:T(8,128)(2,1)} %bitcast.384, f32[4,6,144]{2,1,0:T(8,128)} %get-tuple-element.63, f32[4,6,144,144]{2,3,1,0:T(8,128)} %copy-done.3), kind=kOutput, calls=%fused_computation.72 | convolution fusion | flops 33457680 | bytes 2446848 | tf_op jit(solution)/shard_map/...hqk,...heq->...hek/dot_general | solution.py:211
  205.2 4.3 %reshape.887 = f32[4,6,2,6,1728,1]{4,3,2,1,0,5:T(8,128)S(1)} reshape(f32[4,6,144,144]{3,2,1,0:T(8,128)} %copy.122) | data formatting | bytes 3981312 | tf_op jit(solution)/shard_map/reshape.513
  209.4 6.0 %fusion.22 = f32[4,1,6,2,2,6,138]{6,5,4,3,2,0,1:T(8,128)} fusion(pred[2,138,1728,1,1,1]{2,1,0,3,4,5:T(8,128)(4,1)} %reshape.888, f32[4,6,2,6,1728,1]{4,3,2,1,0,5:T(8,128)S(1)} %reshape.887), kind=kOutput, calls=%fused_computation.41 | convolution fusion | flops 1648263168 | bytes 2785536 | tf_op jit(solution)/shard_map/...rm,gm->...rg/dot_general | solution.py:150
  225.0 4.8 %dynamic_update_slice.4 = f32[1,2,4,2,6,3312]{5,3,4,2,1,0:T(2,128)S(1)} dynamic-update-slice(f32[1,2,4,2,6,3312]{5,3,4,2,1,0:T(2,128)S(1)} %broadcast.593, f32[1,2,4,1,6,3312]{5,3,4,2,1,0:T(1,128)S(1)} %copy.126, s32[]{:T(128)} %constant.96.clone.1, s32[]{:T(128)} %constant.96.clone.1, s32[]{:T(128)} %constant.96.clone.1, s32[]{:T(128)S(6)} %select_n.122, s32[]{:T(128)} %constant.96.clone.1, ...) | dynamic-update-slice | bytes 1271812 | tf_op jit(solution)/shard_map/dynamic_update_slice | solution.py:372
  236.7 18.3 %psum.46 = f32[2,2,192]{2,1,0:T(2,128)S(1)} all-reduce(f32[2,2,192]{2,1,0:T(2,128)S(1)} %pad_maximum_fusion.15), channel_id=1, replica_groups=mesh['section'=4,'lon'=4,'lat'=2] {'lon','lat'}, use_global_device_ids=true, to_apply=%region_30.31 | all-reduce | flops 768 | bytes 6144 | tf_op jit(solution)/shard_map/psum | solution.py:375
  256.4 152.5 %all-reduce.3.cloned.1.call-done = (f32[2,192,576]{2,1,0:T(8,128)}, f32[2,192,192]{2,1,0:T(8,128)}, f32[2,192,768]{2,1,0:T(8,128)}, f32[2,768,192]{1,2,0:T(8,128)}, f32[1,2,4,2,6,3312]{5,3,4,2,1,0:T(2,128)}) async-done(((f32[2,192,576]{2,1,0:T(8,128)}, f32[2,192,192]{2,1,0:T(8,128)}, f32[2,192,768]{2,1,0:T(8,128)}, f32[2,768,192]{1,2,0:T(8,128)}, f32[1,2,4,2,6,3312]{5,3,4,2,1,0:T(2,128)}), ...) | async-done | bytes 4810768 | tf_op jit(solution)/shard_map/psum | solution.py:375
  (394 shorter events, 136.8 us)
Async XLA Ops:
  7.2 401.8 %all-reduce.3.cloned.1.call-start = ((), (), s32[]{:S(2)}) async-start(), calls=%async_computation | async-start | bytes 10027008 | tf_op jit(solution)/shard_map/psum | solution.py:375
  7.3 8.1 %copy-start.102 = (f32[576]{0:T(1024)}, f32[576]{0:T(1024)S(1)}, u32[]{:S(2)}) copy-start(f32[576]{0:T(1024)S(1)} %fusion.139) | copy-start | bytes 6916
  8.1 41.4 %copy-start.99 = (f32[1,1,1,192]{3,2,1,0:T(1,128)}, f32[1,1,1,192]{3,2,1,0:T(1,128)S(1)}, u32[]{:S(2)}) copy-start(f32[1,1,1,192]{3,2,1,0:T(1,128)S(1)} %get-tuple-element.60) | copy-start | bytes 2308
  52.1 57.1 %copy-start = (f32[8,6,12,192]{3,2,1,0:T(8,128)}, f32[8,6,12,192]{3,2,1,0:T(8,128)S(1)}, u32[]{:S(2)}) copy-start(f32[8,6,12,192]{3,2,1,0:T(8,128)S(1)} %get-tuple-element.68) | copy-start | bytes 1327108
  54.2 11.8 %collective-permute-start = (bf16[8,3,12,192]{3,2,1,0:T(8,128)(2,1)}, bf16[8,3,12,192]{3,2,1,0:T(8,128)(2,1)}, u32[]{:S(2)}, u32[]{:S(2)}) collective-permute-start(bf16[8,3,12,192]{3,2,1,0:T(8,128)(2,1)} %get-tuple-element.58), channel_id=1, source_target_pairs={{0,1},{1,0},{2,3},{3,2},{4,5},{5,4},{6,7},{7,6},{8,9},{9,8},{10,11... | collective-permute-start | bytes 331784 | tf_op jit(solution)/shard_map/ppermute | solution.py:27
  68.0 13.4 %collective-permute-start.1 = (bf16[8,6,6,192]{3,2,1,0:T(8,128)(2,1)}, bf16[8,6,6,192]{3,2,1,0:T(8,128)(2,1)}, u32[]{:S(2)}, u32[]{:S(2)}) collective-permute-start(bf16[8,6,6,192]{3,2,1,0:T(8,128)(2,1)} %get-tuple-element.56), channel_id=1, source_target_pairs={{0,6},{2,0},{4,2},{6,4},{1,7},{3,1},{5,3},{7,5},{8,14},{10,8},{12,... | collective-permute-start | bytes 331784 | tf_op jit(solution)/shard_map/ppermute | solution.py:32
  94.5 9.6 %copy-start.13 = (pred[276,12,144]{2,1,0:T(8,128)(4,1)S(1)}, pred[276,12,144]{2,1,0:T(8,128)(4,1)}, u32[]{:S(2)}) copy-start(pred[276,12,144]{2,1,0:T(8,128)(4,1)} %copy-done.12) | copy-start | bytes 1430788
  95.2 12.7 %copy-start.29 = (bf16[1,8,6,12,192]{4,1,3,2,0:T(8,128)(2,1)S(1)}, bf16[1,8,6,12,192]{4,1,3,2,0:T(8,128)(2,1)}, u32[]{:S(2)}) copy-start(bf16[1,8,6,12,192]{4,1,3,2,0:T(8,128)(2,1)} %param.9) | copy-start | bytes 663556
  95.4 7.9 %collective-permute-start.2 = (bf16[8,6,6,192]{3,2,1,0:T(8,128)(2,1)S(1)}, bf16[8,6,6,192]{3,2,1,0:T(8,128)(2,1)S(1)}, u32[]{:S(2)}, u32[]{:S(2)}) collective-permute-start(bf16[8,6,6,192]{3,2,1,0:T(8,128)(2,1)S(1)} %fusion.119), channel_id=1, source_target_pairs={{0,2},{2,4},{4,6},{6,0},{1,3},{3,5},{5,7},{7,1},{8,10},{10,12},{12... | collective-permute-start | bytes 331784 | tf_op jit(solution)/shard_map/ppermute | solution.py:32
  103.5 5.7 %collective-permute-start.3 = (bf16[8,3,12,192]{3,2,1,0:T(8,128)(2,1)S(1)}, bf16[8,3,12,192]{3,2,1,0:T(8,128)(2,1)S(1)}, u32[]{:S(2)}, u32[]{:S(2)}) collective-permute-start(bf16[8,3,12,192]{3,2,1,0:T(8,128)(2,1)S(1)} %get-tuple-element.53), channel_id=1, source_target_pairs={{0,1},{1,0},{2,3},{3,2},{4,5},{5,4},{6,7},{7,6},{8,9},{9,8},{10,11... | collective-permute-start | bytes 331784 | tf_op jit(solution)/shard_map/ppermute | solution.py:27
  115.6 5.7 %collective-permute-start.4 = (bf16[8,3,12,192]{3,2,1,0:T(8,128)(2,1)S(1)}, bf16[8,3,12,192]{3,2,1,0:T(8,128)(2,1)S(1)}, u32[]{:S(2)}, u32[]{:S(2)}) collective-permute-start(bf16[8,3,12,192]{3,2,1,0:T(8,128)(2,1)S(1)} %get-tuple-element.52), channel_id=1, source_target_pairs={{0,1},{1,0},{2,3},{3,2},{4,5},{5,4},{6,7},{7,6},{8,9},{9,8},{10,11... | collective-permute-start | bytes 331784 | tf_op jit(solution)/shard_map/ppermute | solution.py:27
  118.0 9.5 %copy-start.60 = (bf16[1,2,192,192]{3,2,1,0:T(8,128)(2,1)S(1)}, bf16[1,2,192,192]{3,2,1,0:T(8,128)(2,1)}, u32[]{:S(2)}) copy-start(bf16[1,2,192,192]{3,2,1,0:T(8,128)(2,1)} %param.12) | copy-start | bytes 442372
  121.5 5.7 %collective-permute-start.5 = (bf16[8,6,6,192]{3,2,1,0:T(8,128)(2,1)S(1)}, bf16[8,6,6,192]{3,2,1,0:T(8,128)(2,1)S(1)}, u32[]{:S(2)}, u32[]{:S(2)}) collective-permute-start(bf16[8,6,6,192]{3,2,1,0:T(8,128)(2,1)S(1)} %get-tuple-element.50), channel_id=1, source_target_pairs={{0,6},{2,0},{4,2},{6,4},{1,7},{3,1},{5,3},{7,5},{8,14},{10,8},{12,... | collective-permute-start | bytes 331784 | tf_op jit(solution)/shard_map/ppermute | solution.py:32
  161.8 9.4 %copy-start.32 = (bf16[576,192]{1,0:T(8,128)(2,1)S(1)}, bf16[576,192]{1,0:T(8,128)(2,1)}, u32[]{:S(2)}) copy-start(bf16[576,192]{1,0:T(8,128)(2,1)} %copy-done.31) | copy-start | bytes 663556
  161.8 9.4 %copy-start.36 = (bf16[4,1,1,192,144]{3,4,0,2,1:T(8,128)(2,1)S(1)}, bf16[4,1,1,192,144]{3,4,0,2,1:T(8,128)(2,1)}, u32[]{:S(2)}) copy-start(bf16[4,1,1,192,144]{3,4,0,2,1:T(8,128)(2,1)} %copy-done.35) | copy-start | bytes 663556
  162.7 13.7 %copy-start.1 = (f32[8,6,12,192]{3,2,1,0:T(8,128)S(1)}, f32[8,6,12,192]{3,2,1,0:T(8,128)}, u32[]{:S(2)}) copy-start(f32[8,6,12,192]{3,2,1,0:T(8,128)} %copy-done) | copy-start | bytes 1327108
  162.7 13.7 %copy-start.48 = (f32[8,6,12]{2,1,0:T(8,128)S(1)}, f32[8,6,12]{2,1,0:T(8,128)}, u32[]{:S(2)}) copy-start(f32[8,6,12]{2,1,0:T(8,128)} %copy-done.47) | copy-start | bytes 6916
  162.8 7.5 %collective-permute-start.6 = (bf16[8,6,6,192]{3,2,1,0:T(8,128)(2,1)S(1)}, bf16[8,6,6,192]{3,2,1,0:T(8,128)(2,1)S(1)}, u32[]{:S(2)}, u32[]{:S(2)}) collective-permute-start(bf16[8,6,6,192]{3,2,1,0:T(8,128)(2,1)S(1)} %fusion.116), channel_id=1, source_target_pairs={{0,2},{2,4},{4,6},{6,0},{1,3},{3,5},{5,7},{7,1},{8,10},{10,12},{12... | collective-permute-start | bytes 331784 | tf_op jit(solution)/shard_map/ppermute | solution.py:32
  162.9 13.8 %copy-start.90 = (f32[8,6,12]{2,1,0:T(8,128)S(1)}, f32[8,6,12]{2,1,0:T(8,128)}, u32[]{:S(2)}) copy-start(f32[8,6,12]{2,1,0:T(8,128)} %copy-done.89) | copy-start | bytes 6916
  162.9 13.8 %copy-start.76 = (f32[8,6,12]{2,1,0:T(8,128)S(1)}, f32[8,6,12]{2,1,0:T(8,128)}, u32[]{:S(2)}) copy-start(f32[8,6,12]{2,1,0:T(8,128)} %copy-done.75) | copy-start | bytes 6916
  170.5 7.3 %copy-start.15 = (bf16[8,6,12,192]{3,2,1,0:T(8,128)(2,1)S(1)}, bf16[8,6,12,192]{3,2,1,0:T(8,128)(2,1)}, u32[]{:S(2)}) copy-start(bf16[8,6,12,192]{3,2,1,0:T(8,128)(2,1)} %copy-done.14) | copy-start | bytes 663556
  170.6 5.7 %collective-permute-start.7 = (bf16[8,3,12,192]{3,2,1,0:T(8,128)(2,1)S(1)}, bf16[8,3,12,192]{3,2,1,0:T(8,128)(2,1)S(1)}, u32[]{:S(2)}, u32[]{:S(2)}) collective-permute-start(bf16[8,3,12,192]{3,2,1,0:T(8,128)(2,1)S(1)} %get-tuple-element.47), channel_id=1, source_target_pairs={{0,1},{1,0},{2,3},{3,2},{4,5},{5,4},{6,7},{7,6},{8,9},{9,8},{10,11... | collective-permute-start | bytes 331784 | tf_op jit(solution)/shard_map/ppermute | solution.py:27
  209.4 7.8 %copy-start.44 = (f32[1,4,1,6,3312]{4,1,3,2,0:T(4,128)S(1)}, f32[1,4,1,6,3312]{4,1,3,2,0:T(4,128)}, u32[]{:S(2)}) copy-start(f32[1,4,1,6,3312]{4,1,3,2,0:T(4,128)} %copy.157) | copy-start | bytes 953860
  235.3 20.2 %collective-permute-start.8 = (bf16[8,6,12,192]{3,2,1,0:T(8,128)(2,1)S(1)}, bf16[8,6,12,192]{3,2,1,0:T(8,128)(2,1)S(1)}, u32[]{:S(2)}, u32[]{:S(2)}) collective-permute-start(bf16[8,6,12,192]{3,2,1,0:T(8,128)(2,1)S(1)} %add_convert_fusion), channel_id=1, source_target_pairs={{8,0},{16,8},{24,16},{9,1},{17,9},{25,17},{10,2},{18,10},{26,18},{... | collective-permute-start | bytes 663560 | tf_op jit(solution)/shard_map/ppermute | solution.py:38
  (95 other events, 294.4 us)
Sparse Core Ops, SparseCore 0:
  232.3 176.5 all-reduce.2
where the time goes:
time: 432 us; the launch traced here: 423 us
  waiting for transfers between devices  180 us (42%)
  local copies, waits for them, and re-layouts  78.2 us (18%)
  matrix products  77.8 us (18%)
  other arithmetic  43.7 us (10%)
  blocking collectives  18.3 us (4%)
  between operations  16 us (4%)
  starting transfers between devices  9.79 us (2%)
    psum x1, waiting for transfers between devices, on_device(): lax.psum((stacked[0], stacked[1], stacked[2], stacked[3], stacked[4], ful...  153 us
    ppermute x4, waiting for transfers between devices, from_behind(): return lax.ppermute(x, axis, [(i, (i + by) % size) for i in range(size)])  18.4 us
    psum x1, blocking collectives, on_device(): lax.psum((stacked[0], stacked[1], stacked[2], stacked[3], stacked[4], ful...  18.3 us
    dot_general x2, matrix products, table_grad(): jnp.einsum('...rm,gm->...rg', shaped, spread_map, precision=lax.Precision...  11.9 us
    dot_general x8, matrix products, grad_weight(): lax.dot_general(token_rows, grad_rows, (((0,), (0,)), ((), ())), preferre...  11.6 us
    another operation x6, local copies, waits for them, and re-layouts  10.1 us
    dot_general x2, matrix products, attend_backward(): jnp.einsum('...hqk,...heq->...hek', weights, grad_mixture, preferred_elem...  9.94 us
    reshape x2, local copies, waits for them, and re-layouts, dense_bias(): bias_dense = spread.reshape(leading + (WIN_TOKENS, WIN_TOKENS))  8.79 us
  transfers between devices with their start and end apart: 10, of which 7 were waited for; matrix products, arithmetic and copies ran while one was open for 7% of the time, Pallas kernels for 0%

commit v1 on v0

v1 whole, which is shorter than its diff:
```python
import functools

import jax
import jax.numpy as jnp
import numpy as np
from jax import lax
from jax.experimental import pallas as pl
from jax.experimental.pallas import tpu as pltpu
from jax.sharding import PartitionSpec as P

D = 192
HEADS = 6
HEAD_SIZE = 32
LEVELS = 8
WIN_LEVELS = 2
ROWS = 6
COLS = 12
WIN = 144
LEVEL_WINDOWS = 4
TOKENS = 576
MLP = 768
SLOTS = 3312
GROUPS = 12
OFFSETS = 23
PAIRS = GROUPS * OFFSETS
PAIRS_PAD = 384
STACK = HEADS * WIN
TABLE_ROWS = LEVEL_WINDOWS * HEADS * GROUPS
TABLE_PAD = 320
GRAD_LANES = 2560
NORM_EPS = 1e-05
MASK_FILL = -10000.0
Q_SCALE = HEAD_SIZE ** (-0.5)
VMEM_BYTES = 50 * 1024 * 1024
F32 = jnp.float32
BF16 = jnp.bfloat16
DENSE = 288


def roll_maps():
    split = np.zeros((TOKENS, TOKENS), np.float32)
    join = np.zeros((TOKENS, TOKENS), np.float32)
    row = 0
    for dest in range(4):
        for level in range(LEVELS):
            for r in range(3):
                for c in range(6):
                    src_r = (1 - dest // 2) * 3 + r
                    src_c = (1 - dest % 2) * 6 + c
                    src = ((level + 1) % LEVELS) * 72 + src_r * COLS + src_c
                    split[row, src] = 1
                    out = level * 72 + ((dest // 2) * 3 + r) * COLS + (dest % 2) * 6 + c
                    join[out, row] = 1
                    row += 1
    return split, join


def spread_map():
    table = np.zeros((COLS, PAIRS_PAD, 256), np.float32)
    for cq in range(COLS):
        for key in range(WIN):
            group, ck = key // COLS, key % COLS
            table[cq, group * OFFSETS + cq - ck + COLS - 1, key] = 1
    return table


def mm(a, b):
    return jnp.dot(a, b, preferred_element_type=F32)


def mm_bt(a, b):
    return lax.dot_general(a, b, (((1,), (1,)), ((), ())), preferred_element_type=F32)


def mm_at(a, b):
    return lax.dot_general(a, b, (((0,), (0,)), ((), ())), preferred_element_type=F32)


def norm_parts(v):
    centred = v - jnp.mean(v, axis=-1, keepdims=True)
    rstd = lax.rsqrt(jnp.mean(centred * centred, axis=-1, keepdims=True) + NORM_EPS)
    return centred * rstd, rstd


def norm_back(v, gain, grad):
    hat, rstd = norm_parts(v)
    scaled = grad * gain
    m1 = jnp.mean(scaled, axis=-1, keepdims=True)
    m2 = jnp.mean(scaled * hat, axis=-1, keepdims=True)
    return rstd * (scaled - m1 - hat * m2), jnp.sum(grad * hat, axis=0, keepdims=True)


def gelu_both(u):
    c = 0.7978845608028654
    t = jnp.tanh(c * (u + 0.044715 * (u * u * u)))
    value = 0.5 * u * (1.0 + t)
    slope = 0.5 * (1.0 + t) + 0.5 * u * (1.0 - t * t) * (c * (1.0 + 3 * 0.044715 * (u * u)))
    return value, slope


def head_masks(dtype):
    lane = lax.broadcasted_iota(jnp.int32, (1, D), 1)
    return [
        jnp.where((lane >= h * HEAD_SIZE) & (lane < (h + 1) * HEAD_SIZE), 1.0, 0.0).astype(dtype)
        for h in range(HEADS)
    ]


def stack_heads(x):
    return jnp.concatenate([x * m for m in head_masks(BF16)], axis=0)


def merge_heads(x):
    total = None
    for h, m in enumerate(head_masks(F32)):
        part = x[h * WIN : (h + 1) * WIN] * m
        total = part if total is None else total + part
    return total


def dense_loop(fn):
    def step(i, carry):
        fn(pl.ds(pl.multiple_of(i * DENSE, 16), DENSE))
        return carry

    lax.fori_loop(0, TOKENS // DENSE, step, 0)


def split3(x):
    hi = x.astype(BF16)
    rest = x - hi.astype(F32)
    mid = rest.astype(BF16)
    low = (rest - mid.astype(F32)).astype(BF16)
    return hi, mid, low


def bias_build(table_ref, spread_ref, ba, bb):
    hi, mid, low = split3(table_ref[...])
    for cq in range(COLS):
        s = spread_ref[cq]
        r = (mm(low, s) + mm(mid, s)) + mm(hi, s)
        ba[pl.ds(cq, TABLE_ROWS, COLS), :] = r[:, :128]
        bb[pl.ds(cq, TABLE_ROWS, COLS), :] = r[:, 128:]


def table_fold(ga, gb, spread_ref, out_ref, gains):
    acc = jnp.zeros((TABLE_ROWS, PAIRS_PAD), F32)
    for cq in range(COLS):
        x = jnp.concatenate(
            [ga[pl.ds(cq, TABLE_ROWS, COLS), :], gb[pl.ds(cq, TABLE_ROWS, COLS), :]], axis=1
        )
        hi = x.astype(BF16)
        low = (x - hi.astype(F32)).astype(BF16)
        s = spread_ref[cq]
        acc = acc + (mm_bt(low, s) + mm_bt(hi, s))
    out_ref[0:TABLE_ROWS, :] = acc.astype(BF16)


def project(framed, wi_ref, q_ref, k_ref, v_ref, rows):
    q_ref[rows, :] = (mm(framed, wi_ref[0]) * Q_SCALE).astype(BF16)
    k_ref[rows, :] = mm(framed, wi_ref[1]).astype(BF16)
    v_ref[rows, :] = mm(framed, wi_ref[2]).astype(BF16)


def attend(q_ref, k_ref, v_ref, ba, bb, at_ref, mx_ref, last_band):
    def window(w, carry):
        rows = pl.ds(pl.multiple_of(w * WIN, 16), WIN)
        big = pl.ds(pl.multiple_of(w * STACK, 16), STACK)
        qst = stack_heads(q_ref[rows, :])
        scores = mm_bt(qst, k_ref[rows, :])
        scores = scores + jnp.concatenate([ba[big, :], bb[big, :]], axis=1)[:, :WIN]
        if last_band is not None:
            qi = lax.broadcasted_iota(jnp.int32, (WIN, WIN), 0)
            ki = lax.broadcasted_iota(jnp.int32, (WIN, WIN), 1)
            qa, ka = (qi >= 72).astype(jnp.int32), (ki >= 72).astype(jnp.int32)
            qb = (qi - 72 * qa >= 36).astype(jnp.int32)
            kb = (ki - 72 * ka >= 36).astype(jnp.int32)
            last_level = (w == LEVEL_WINDOWS - 1).astype(jnp.int32)
            apart = (qa != ka).astype(jnp.int32) * last_level + (qb != kb).astype(
                jnp.int32
            ) * last_band
            mask = jnp.where(apart > 0, MASK_FILL, 0.0)
            scores = scores + jnp.concatenate([mask] * HEADS, axis=0)
        scores = jnp.exp(scores - jnp.max(scores, axis=-1, keepdims=True))
        att = scores / jnp.sum(scores, axis=-1, keepdims=True)
        at_ref[big, :] = att
        mx_ref[rows, :] = merge_heads(mm(att.astype(BF16), v_ref[rows, :])).astype(BF16)
        return carry

    lax.fori_loop(0, LEVEL_WINDOWS, window, 0)


def attend_back(q_ref, k_ref, v_ref, at_ref, gmx, gq_ref, gk_ref, gv_ref, ga, gb):
    def window(w, carry):
        rows = pl.ds(pl.multiple_of(w * WIN, 16), WIN)
        big = pl.ds(pl.multiple_of(w * STACK, 16), STACK)
        qst = stack_heads(q_ref[rows, :])
        gst = stack_heads(gmx[rows, :])
        att = at_ref[big, :]
        gv_ref[rows, :] = mm_at(att.astype(BF16), gst).astype(BF16)
        gw = mm_bt(gst, v_ref[rows, :])
        gs = att * (gw - jnp.sum(att * gw, axis=-1, keepdims=True))
        ga[big, :] = gs[:, :128]
        gb[big, :] = jnp.concatenate([gs[:, 128:], jnp.zeros((STACK, 256 - WIN), F32)], axis=1)
        sp = gs.astype(BF16)
        gq_ref[rows, :] = (merge_heads(mm(sp, k_ref[rows, :])) * Q_SCALE).astype(BF16)
        gk_ref[rows, :] = mm_at(sp, qst).astype(BF16)
        return carry

    lax.fori_loop(0, LEVEL_WINDOWS, window, 0)


def bias_kernel(table_ref, spread_ref, ba, bb):
    bias_build(table_ref, spread_ref, ba, bb)


def forward0_kernel(
    x, gains, wi, wo, we, wr, table, spread, split,
    fr, q, k, v, at, mx, md, nm, hb, gd, a1, sq,
    ba, bb, n1,
):
    bias_build(table, spread, ba, bb)

    def first(rows):
        framed = (norm_parts(x[rows, :].astype(F32))[0] * gains[0:1, :]).astype(BF16)
        fr[rows, :] = framed
        project(framed, wi, q, k, v, rows)

    dense_loop(first)
    attend(q, k, v, ba, bb, at, mx, None)

    def second(rows):
        mid = (x[rows, :].astype(F32) + mm(mx[rows, :], wo[...])).astype(BF16)
        md[rows, :] = mid
        midf = mid.astype(F32)
        normed = (norm_parts(midf)[0] * gains[1:2, :]).astype(BF16)
        nm[rows, :] = normed
        hidden, slope = gelu_both(mm(normed, we[...]))
        hidden = hidden.astype(BF16)
        hb[rows, :] = hidden
        gd[rows, :] = slope.astype(BF16)
        out = (midf + mm(hidden, wr[...])).astype(BF16)
        a1[rows, :] = out
        n1[rows, :] = (norm_parts(out.astype(F32))[0] * gains[2:3, :]).astype(BF16)

    dense_loop(second)
    sq[...] = mm(split[...], n1[...]).astype(BF16)


def forward1_kernel(rq, wi, wo, ba, bb, join, join_t, fr, q, k, v, at, mx, out, *, lat_name):
    def first(rows):
        framed = mm(join[rows, :], rq[...]).astype(BF16)
        fr[rows, :] = framed
        project(framed, wi, q, k, v, rows)

    dense_loop(first)
    last_band = (lax.axis_index(lat_name) == lax.axis_size(lat_name) - 1).astype(jnp.int32)
    attend(q, k, v, ba, bb, at, mx, last_band)
    attended = mm(mx[...], wo[...]).astype(BF16)
    out[...] = mm(join_t[...], attended).astype(BF16)


def mlp_back(rows, e, md, gd, gain, we, wr, gp):
    ef = e[rows, :]
    pre = (gd[rows, :].astype(F32) * mm_bt(ef, wr[...])).astype(BF16)
    gp[rows, :] = pre
    dx, dg = norm_back(md[rows, :].astype(F32), gain, mm_bt(pre, we[...]))
    return ef.astype(F32) + dx, dg


def middle1_kernel(
    rq, a1, go, gains, we, wr, split, split_t,
    gm, gmlp, gain_out, sq,
    md, nm, hb, gd, gp, gmb,
):
    gain_out[...] = jnp.zeros_like(gain_out)

    def step(rows):
        attended = mm(split_t[rows, :], rq[...])
        mid = (a1[rows, :].astype(F32) + attended).astype(BF16)
        md[rows, :] = mid
        normed = (norm_parts(mid.astype(F32))[0] * gains[3:4, :]).astype(BF16)
        nm[rows, :] = normed
        hidden, slope = gelu_both(mm(normed, we[...]))
        hb[rows, :] = hidden.astype(BF16)
        gd[rows, :] = slope.astype(BF16)
        grad, dg = mlp_back(rows, go, md, gd, gains[3:4, :], we, wr, gp)
        gm[rows, :] = grad
        gmb[rows, :] = grad.astype(BF16)
        gain_out[0:1, :] += dg

    dense_loop(step)
    sq[...] = mm(split[...], gmb[...]).astype(BF16)
    gmlp[:, 0:MLP] = mm_at(nm[...], gp[...]).astype(BF16)
    gmlp[:, MLP:] = mm_at(go[...], hb[...]).astype(BF16)


def attention_grads(fr, mx, grad_att, gq, gk, gv, g_out):
    pad = jnp.zeros((D, 64), F32)
    parts = [
        mm_at(fr[...], gq[...]),
        mm_at(fr[...], gk[...]),
        mm_at(fr[...], gv[...]),
        mm_at(mx[...], grad_att),
    ]
    for i, part in enumerate(parts):
        g_out[:, i * 256 : (i + 1) * 256] = jnp.concatenate([part, pad], axis=1).astype(BF16)


def back1_kernel(
    rq, gmlp, fr, q, k, v, at, mx, wi, wo, join, join_t,
    g_out, out, ga, gb,
    gatt, gmx, gq, gk, gv,
):
    def first(rows):
        moved = mm(join[rows, :], rq[...]).astype(BF16)
        gatt[rows, :] = moved
        gmx[rows, :] = mm_bt(moved, wo[...]).astype(BF16)

    dense_loop(first)
    attend_back(q, k, v, at, gmx, gq, gk, gv, ga, gb)
    gn = mm_bt(gq[...], wi[0]) + mm_bt(gk[...], wi[1]) + mm_bt(gv[...], wi[2])
    out[...] = mm(join_t[...], gn.astype(BF16)).astype(BF16)
    attention_grads(fr, mx, gatt[...], gq, gk, gv, g_out)
    g_out[:, 1024:] = gmlp[...]


def table_kernel(ga, gb, spread, out):
    table_fold(ga, gb, spread, out, None)
    out[TABLE_ROWS:, :] = jnp.zeros((TABLE_PAD - TABLE_ROWS, PAIRS_PAD), BF16)


def back0_kernel(
    rq, gm1, a1, x, gains, gain_in, fr, q, k, v, at, mx, md, nm, hb, gd, wi, wo, we, wr,
    spread, split_t,
    g_out, e0, t_out,
    e1, gp, gm0, gatt, gmx, gq, gk, gv, ga, gb, dgains,
):
    dgains[...] = jnp.zeros_like(dgains)
    dgains[3:4, 0:D] = gain_in[0:1, :]

    def first(rows):
        moved = mm(split_t[rows, :], rq[...])
        dx, dg = norm_back(a1[rows, :].astype(F32), gains[2:3, :], moved)
        e1[rows, :] = (gm1[rows, :] + dx).astype(BF16)
        dgains[2:3, 0:D] += dg
        grad, dg = mlp_back(rows, e1, md, gd, gains[1:2, :], we, wr, gp)
        dgains[1:2, 0:D] += dg
        gm0[rows, :] = grad
        moved = grad.astype(BF16)
        gatt[rows, :] = moved
        gmx[rows, :] = mm_bt(moved, wo[...]).astype(BF16)

    dense_loop(first)
    attend_back(q, k, v, at, gmx, gq, gk, gv, ga, gb)

    def last(rows):
        gn = mm_bt(gq[rows, :], wi[0]) + mm_bt(gk[rows, :], wi[1]) + mm_bt(gv[rows, :], wi[2])
        gn = gn.astype(BF16).astype(F32)
        dx, dg = norm_back(x[rows, :].astype(F32), gains[0:1, :], gn)
        dgains[0:1, 0:D] += dg
        e0[rows, :] = (gm0[rows, :] + dx).astype(BF16)

    dense_loop(last)
    attention_grads(fr, mx, gatt[...], gq, gk, gv, g_out)
    g_out[:, 1024 : 1024 + MLP] = mm_at(nm[...], gp[...]).astype(BF16)
    g_out[:, 1024 + MLP :] = mm_at(e1[...], hb[...]).astype(BF16)
    table_fold(ga, gb, spread, t_out, None)
    t_out[TABLE_ROWS:, :] = dgains[...].astype(BF16)


def bf(*shape):
    return jax.ShapeDtypeStruct(shape, BF16)


def ff(*shape):
    return jax.ShapeDtypeStruct(shape, F32)


def run(body, args, outs, scratch=(), flops=10**9):
    return pl.pallas_call(
        body,
        out_shape=tuple(outs),
        in_specs=[pl.BlockSpec(memory_space=pltpu.VMEM)] * len(args),
        out_specs=tuple(pl.BlockSpec(memory_space=pltpu.VMEM) for _ in outs),
        scratch_shapes=[pltpu.VMEM(s.shape, s.dtype) for s in scratch],
        compiler_params=pltpu.CompilerParams(vmem_limit_bytes=VMEM_BYTES),
        cost_estimate=pl.CostEstimate(flops=flops, bytes_accessed=10**7, transcendentals=0),
    )(*args)


def exchange(quads, step):
    lon_n, lat_n = lax.axis_size("lon"), lax.axis_size("lat")

    def moved(part, dlat, dlon):
        pairs = []
        for lo in range(lon_n):
            for la in range(lat_n):
                dest = ((lo + dlon) % lon_n) * lat_n + (la + dlat) % lat_n
                pairs.append((lo * lat_n + la, dest))
        return lax.ppermute(part, ("lon", "lat"), pairs)

    parts = [quads[i * WIN : (i + 1) * WIN] for i in range(4)]
    return jnp.concatenate(
        [parts[0], moved(parts[1], 0, step), moved(parts[2], 1, 0), moved(parts[3], 1, step)],
        axis=0,
    )


def reduce_all(grads, table):
    total = lax.psum(grads, ("lon", "lat"))
    table = lax.psum(table, "lon")
    return total, lax.all_gather(table, "lat", axis=0)


def on_device(
    inputs, grad_output, norm_gains, input_weight, output_weight, expand_weight, reduce_weight,
    bias_table,
):
    lat_index = lax.axis_index("lat")
    lat_total = ROWS * lax.axis_size("lat")
    split_np, join_np = roll_maps()
    split, split_t = jnp.asarray(split_np, BF16), jnp.asarray(split_np.T, BF16)
    join, join_t = jnp.asarray(join_np, BF16), jnp.asarray(join_np.T, BF16)
    spread = jnp.asarray(spread_map(), BF16)
    x = inputs.reshape(TOKENS, D)
    go = grad_output.reshape(TOKENS, D)
    gains = norm_gains.reshape(4, D)
    wi = input_weight[0].reshape(2, D, 3, D).swapaxes(1, 2)
    wo, we, wr = output_weight[0], expand_weight[0], reduce_weight[0]
    rows = lax.dynamic_slice_in_dim(bias_table[0], lat_index, 1, axis=2)[:, :, 0]
    rows = rows.reshape(2, LEVEL_WINDOWS * HEADS, 2, 2, 6, 6 * OFFSETS).swapaxes(3, 4)
    rows = rows.reshape(2, TABLE_ROWS, PAIRS)
    rows = jnp.pad(rows, ((0, 0), (0, 0), (0, PAIRS_PAD - PAIRS)))

    big = LEVEL_WINDOWS * STACK
    tok = bf(TOKENS, D)
    wide = bf(TOKENS, MLP)
    half_bias = [ff(big, 128)] * 2
    fr0, q0, k0, v0, at0, mx0, md0, nm0, hb0, gd0, a1, sq = run(
        forward0_kernel,
        (x, gains, wi[0], wo[0], we[0], wr[0], rows[0], spread, split),
        (tok, tok, tok, tok, ff(big, WIN), tok, tok, tok, wide, wide, tok, tok),
        (*half_bias, tok),
    )
    ba, bb = run(bias_kernel, (rows[1], spread), half_bias)
    rq = exchange(sq, -1)
    fr1, q1, k1, v1, at1, mx1, oq = run(
        functools.partial(forward1_kernel, lat_name="lat"),
        (rq, wi[1], wo[1], ba, bb, join, join_t),
        (tok, tok, tok, tok, ff(big, WIN), tok, tok),
    )
    rq = exchange(oq, 1)
    gm1, gmlp, dgain, sq = run(
        middle1_kernel,
        (rq, a1, go, gains, we[1], wr[1], split, split_t),
        (ff(TOKENS, D), bf(D, 2 * MLP), ff(8, D), tok),
        (tok, tok, wide, wide, wide, tok),
    )
    rq = exchange(sq, -1)
    g1, oq, ga, gb = run(
        back1_kernel,
        (rq, gmlp, fr1, q1, k1, v1, at1, mx1, wi[1], wo[1], join, join_t),
        (bf(D, GRAD_LANES), tok, *half_bias),
        (tok, tok, tok, tok, tok),
    )
    (t1,) = run(table_kernel, (ga, gb, spread), (bf(TABLE_PAD, PAIRS_PAD),))
    rq = exchange(oq, 1)
    g0, e0, t0 = run(
        back0_kernel,
        (rq, gm1, a1, x, gains, dgain, fr0, q0, k0, v0, at0, mx0, md0, nm0, hb0, gd0,
         wi[0], wo[0], we[0], wr[0], spread, split_t),
        (bf(D, GRAD_LANES), tok, bf(TABLE_PAD, PAIRS_PAD)),
        (tok, wide, ff(TOKENS, D), tok, tok, tok, tok, tok, *half_bias, ff(32, PAIRS_PAD)),
    )
    sections = lax.axis_size("section")
    upstream = lax.ppermute(e0, "section", [(i, i - 1) for i in range(1, sections)])
    sum1, sum0, tables = reduce_grads(g0, g1, t0, t1)
    return finish(upstream, sum0, sum1, tables, lat_total, inputs.shape)


def reduce_grads(g0, g1, t0, t1):
    sum1 = lax.psum(g1, ("lon", "lat"))
    sum0 = lax.psum(g0, ("lon", "lat"))
    tables = lax.all_gather(lax.psum(jnp.stack([t0, t1]), "lon"), "lat", axis=0)
    return sum1, sum0, tables


def finish(upstream, sum0, sum1, tables, lat_total, shape):
    grad_scale = float(LEVELS * lat_total * COLS * lax.axis_size("lon")) ** (-0.5)
    lat_n = tables.shape[0]
    sums = jnp.stack([sum0, sum1]).astype(F32) * grad_scale
    wi_g = jnp.concatenate([sums[:, :, i * 256 : i * 256 + D] for i in range(3)], axis=-1)
    wo_g = sums[:, :, 768 : 768 + D]
    we_g = sums[:, :, 1024 : 1024 + MLP]
    wr_g = sums[:, :, 1024 + MLP :].swapaxes(1, 2)
    gains = tables[:, 0, TABLE_ROWS : TABLE_ROWS + 4, :D].astype(F32).sum(0) * grad_scale
    tab = tables[:, :, :TABLE_ROWS, :PAIRS]
    tab = tab.reshape(lat_n, 2, LEVEL_WINDOWS, HEADS, 2, 6, 2, 6 * OFFSETS)
    tab = tab.transpose(1, 2, 0, 3, 4, 6, 5, 7)
    tab = tab.reshape(1, 2, LEVEL_WINDOWS, lat_n, HEADS, SLOTS).astype(F32)
    return (
        upstream.reshape(shape),
        wi_g[None],
        wo_g[None],
        we_g[None],
        wr_g[None],
        gains.reshape(1, 2, 2, D),
        tab,
    )


def solution(mesh):
    token = P("section", None, "lat", "lon", None)
    weight = P("section", None, None, None)
    table = P("section", None, None, None, None, None)
    return jax.shard_map(
        on_device,
        mesh=mesh,
        in_specs=(token, token, weight, weight, weight, weight, weight, table),
        out_specs=(token, weight, weight, weight, weight, weight, table),
        check_vma=False,
    )
```

time: 432 us -> 282 us (0.65); the launches traced: 423 us -> 282 us
  matrix products: 77.8 us -> 0 us
  waiting for transfers between devices: 180 us -> 122 us
  Pallas kernels: 0 us -> 57.4 us
  other arithmetic: 43.7 us -> 5.23 us
  local copies, waits for them, and re-layouts: 78.2 us -> 49.2 us
  starting transfers between devices: 9.79 us -> 16.8 us
    dot_general x39 -> x0, matrix products: 77.8 us -> none  [the longest x2 11.9 us: table_grad(): jnp.einsum('...rm,gm->...rg', shaped, spread_map, precision=lax.Precision...]
    pallas_call x0 -> x7, Pallas kernels: none -> 57.4 us  [run(): pl.pallas_call(body, out_shape=tuple(outs), in_specs=[pl.BlockSpec(memory...]
    psum x1 -> x2, waiting for transfers between devices: 153 us -> 111 us  [the longest x1 76.9 us: reduce_grads(): sum1 = lax.psum(g1, ('lon', 'lat'))]
    psum x1 -> x0, blocking collectives: 18.3 us -> none  [on_device(): lax.psum((stacked[0], stacked[1], stacked[2], stacked[3], stacked[4], ful...]
    another operation x18 -> x2, local copies, waits for them, and re-layouts: 21.3 us -> 3.95 us  [the longest x1 2.86 us: on_device(): rows.reshape(2, LEVEL_WINDOWS * HEADS, 2, 2, 6, 6 * OFFSETS).swapaxes(3, 4)]
    ppermute x9 -> x13, waiting for transfers between devices: 27.2 us -> 10.6 us  [the longest x12 8.38 us: moved(): return lax.ppermute(part, ('lon', 'lat'), pairs)]
    all_gather x0 -> x1, blocking collectives: none -> 16.2 us  [reduce_grads(): tables = lax.all_gather(lax.psum(jnp.stack([t0, t1]), 'lon'), 'lat', axis=0)]
    reshape x9 -> x5, local copies, waits for them, and re-layouts: 13.9 us -> 3.8 us  [the longest x1 1.93 us: on_device(): rows = rows.reshape(2, TABLE_ROWS, PAIRS)]
  transfers between devices with their start and end apart: 10 -> 15, of which waited for: 7 -> 9; matrix products, arithmetic and copies ran while one was open for 7% -> 5% of each run, Pallas kernels for 0% -> 3%
where the time goes in v1:
time: 282 us
  waiting for transfers between devices  122 us (43%)
  Pallas kernels  57.4 us (20%)
  local copies, waits for them, and re-layouts  49.2 us (17%)
  starting transfers between devices  16.8 us (6%)
  blocking collectives  16.2 us (6%)
  between operations  14.5 us (5%)
  other arithmetic  5.23 us (2%)
    psum x1, waiting for transfers between devices, reduce_grads(): sum1 = lax.psum(g1, ('lon', 'lat'))  76.9 us
    pallas_call x7, Pallas kernels, run(): pl.pallas_call(body, out_shape=tuple(outs), in_specs=[pl.BlockSpec(memory...  57.4 us
    psum x1, waiting for transfers between devices, reduce_grads(): tables = lax.all_gather(lax.psum(jnp.stack([t0, t1]), 'lon'), 'lat', axis=0)  34.2 us
    unnamed x92, local copies, waits for them, and re-layouts  18.8 us
    all_gather x1, blocking collectives, reduce_grads(): tables = lax.all_gather(lax.psum(jnp.stack([t0, t1]), 'lon'), 'lat', axis=0)  16.2 us
    ppermute x12, starting transfers between devices, moved(): return lax.ppermute(part, ('lon', 'lat'), pairs)  15.4 us
    convert_element_type x3, local copies, waits for them, and re-layouts, finish(): tab = tab.reshape(1, 2, LEVEL_WINDOWS, lat_n, HEADS, SLOTS).astype(F32)  9.14 us
    ppermute x12, waiting for transfers between devices, moved(): return lax.ppermute(part, ('lon', 'lat'), pairs)  8.38 us
  transfers between devices with their start and end apart: 15, of which 9 were waited for; matrix products, arithmetic and copies ran while one was open for 5% of the time, Pallas kernels for 3%

profile of v1, /device:TPU:0, one launch (start us, length us, event | category | flops | bytes accessed | tf_op | source)
XLA Modules:
  0.0 281.8 jit_solution(10895852952054114723)
XLA Ops:
  17.5 2.9 %reshape_squeeze.7 = f32[2,24,2,2,6,138]{5,4,3,2,0,1:T(8,128)} reshape(f32[1,2,4,1,6,3312]{5,1,4,2,3,0:T(2,128)S(1)} %copy.40) | data formatting | bytes 1271808 | tf_op jit(solution)/shard_map/reshape;squeeze | solution.py:432
  20.4 2.0 copy.41
  22.4 1.9 reshape.77
  24.3 2.0 fusion.1
  26.3 13.3 %shard_map.180 = (bf16[576,192]{1,0:T(8,128)(2,1)S(1)}, bf16[576,192]{1,0:T(8,128)(2,1)S(1)}, bf16[576,192]{1,0:T(8,128)(2,1)S(1)}, bf16[576,192]{1,0:T(8,128)(2...) custom-call(bf16[576,192]{1,0:T(8,128)(2,1)S(1)} %reshape.75.x, ...), custom_call_target="tpu_custom_call" | custom-call | flops 1000000000 | bytes 10000000 | tf_op jit(solution)/shard_map/pallas_call | solution.py:381
  43.9 6.1 %collective-permute-start.2 = (bf16[144,192]{1,0:T(8,128)(2,1)S(1)}, bf16[144,192]{1,0:T(8,128)(2,1)S(1)}, u32[]{:S(2)}, u32[]{:S(2)}) collective-permute-start(bf16[144,192]{1,0:T(8,128)(2,1)S(1)} %get-tuple-element.121), channel_id=1, source_target_pairs={{0,7},{1,6},{2,1},{3,0},{4,3},{5,2},{6,5},{7,4},{8,15},{9,14},{10,... | collective-permute-start | bytes 165896 | tf_op jit(solution)/shard_map/ppermute | solution.py:401
  51.0 4.7 %shard_map.181 = (f32[3456,128]{1,0:T(8,128)S(1)}, f32[3456,128]{1,0:T(8,128)S(1)}) custom-call(f32[288,384]{1,0:T(8,128)S(1)} %get-tuple-element.100.table_ref, bf16[12,384,256]{2,1,0:T(8,128)(2,1)} %constant.29.clone.spread.spread_ref), custom_call_target="tpu_custom_call" | custom-call | flops 1000000000 | bytes 10000000 | tf_op jit(solution)/shard_map/pallas_call | solution.py:381
  58.3 8.4 %shard_map.182 = (bf16[576,192]{1,0:T(8,128)(2,1)S(1)}, bf16[576,192]{1,0:T(8,128)(2,1)S(1)}, bf16[576,192]{1,0:T(8,128)(2,1)S(1)}, bf16[576,192]{1,0:T(8,128)(2...) custom-call(bf16[576,192]{1,0:T(8,128)(2,1)S(1)} %pad_maximum_fusion.rq, ...), custom_call_target="tpu_custom_call" | custom-call | flops 1000000000 | bytes 10000000 | tf_op jit(solution)/shard_map/pallas_call | solution.py:381
  69.8 2.5 collective-permute-start.5
  74.9 2.6 collective-permute-done.5
  82.0 5.3 %shard_map.183 = (f32[576,192]{1,0:T(8,128)S(1)}, bf16[192,1536]{1,0:T(8,128)(2,1)S(1)}, f32[8,192]{1,0:T(8,128)S(1)}, bf16[576,192]{1,0:T(8,128)(2,1)S(1)}) custom-call(bf16[576,192]{1,0:T(8,128)(2,1)S(1)} %pad_maximum_fusion.1.rq, bf16[576,192]{1,0:T(8,128)(2,1)S(1)} %copy-done.29, bf16[576,192]{1,0:T(8,128)(2,1)S(1)} %copy-done.13, ...), custom_call_target="tpu_custom_call" | custom-call | flops 1000000000 | bytes 10000000 | tf_op jit(solution)/shard_map/pallas_call | solution.py:381
  89.4 3.2 %collective-permute-done.8 = bf16[144,192]{1,0:T(8,128)(2,1)S(1)} collective-permute-done((bf16[144,192]{1,0:T(8,128)(2,1)S(1)}, bf16[144,192]{1,0:T(8,128)(2,1)S(1)}, u32[]{:S(2)}, u32[]{:S(2)}) %collective-permute-start.8) | collective-permute-done | bytes 55328 | tf_op jit(solution)/shard_map/ppermute | solution.py:401
  93.8 9.3 %shard_map.184 = (bf16[192,2560]{1,0:T(8,128)(2,1)}, bf16[576,192]{1,0:T(8,128)(2,1)S(1)}, f32[3456,128]{1,0:T(8,128)}, f32[3456,128]{1,0:T(8,128)}) custom-call(bf16[576,192]{1,0:T(8,128)(2,1)S(1)} %pad_maximum_fusion.2.rq, bf16[192,1536]{1,0:T(8,128)(2,1)S(1)} %get-tuple-element.45.gmlp, bf16[576,192]{1,0:T(8,128)(2,1)S(1)} %copy-done.32, ...), custom_call_target="tpu_custom_call" | custom-call | flops 1000000000 | bytes 10000000 | tf_op jit(solution)/shard_map/pallas_call | solution.py:381
  103.1 2.6 collective-permute-start.11
  109.3 3.8 %shard_map.186 = bf16[320,384]{1,0:T(8,128)(2,1)S(1)} custom-call(f32[3456,128]{1,0:T(8,128)S(1)} %copy-done.6, f32[3456,128]{1,0:T(8,128)S(1)} %copy-done.7, bf16[12,384,256]{2,1,0:T(8,128)(2,1)} %constant.29.clone.spread.spread_ref), custom_call_target="tpu_custom_call" | custom-call | flops 1000000000 | bytes 10000000 | tf_op jit(solution)/shard_map/pallas_call | solution.py:381
  113.3 12.7 %shard_map.185 = (bf16[192,2560]{1,0:T(8,128)(2,1)}, bf16[576,192]{1,0:T(8,128)(2,1)S(1)}, bf16[320,384]{1,0:T(8,128)(2,1)S(1)}) custom-call(bf16[576,192]{1,0:T(8,128)(2,1)S(1)} %pad_maximum_fusion.3.rq, f32[576,192]{1,0:T(8,128)} %copy-done.11, bf16[576,192]{1,0:T(8,128)(2,1)S(1)} %copy-done.30, bf16[576,192]{1,0:T(8,128)(2,1)S(1)} %reshape.75.x, ...), custom_call_target="tpu_custom_call" | custom-call | flops 1000000000 | bytes 10000000 | tf_op jit(solution)/shard_map/pallas_call | solution.py:381
  128.9 2.2 collective-permute-done.12
  132.0 34.2 %all-reduce.5.cloned.1.call-done = bf16[1,2,320,384]{3,2,1,0:T(8,128)(2,1)} async-done(((bf16[1,2,320,384]{3,2,1,0:T(8,128)(2,1)}), bf16[1,2,320,384]{3,2,1,0:T(8,128)(2,1)}) %all-reduce.5.cloned.1.call-update) | async-done | bytes 491536 | tf_op jit(solution)/shard_map/psum | solution.py:485
  166.2 16.2 %all_gather.7 = bf16[2,2,320,384]{3,2,1,0:T(8,128)(2,1)S(1)} all-gather(bf16[1,2,320,384]{3,2,1,0:T(8,128)(2,1)} %all-reduce.5.cloned.1.call-done), channel_id=1, replica_groups=mesh['section'=4,'lon'=4,'lat'=2] {'lat'}, dimensions={0}, use_global_device_ids=true | all-gather | bytes 1474560 | tf_op jit(solution)/shard_map/all_gather | solution.py:485
  183.2 3.4 %reshape.81 = f32[2,2,4,6,2,6,2,138]{7,6,5,4,3,2,1,0:T(2,128)} reshape(f32[2,2,288,276]{3,2,1,0:T(8,128)S(1)} %slice_convert_fusion) | data formatting | bytes 2543616 | tf_op jit(solution)/shard_map/convert_element_type | solution.py:501
  186.6 2.2 copy.44
  188.8 3.5 %reshape.80 = f32[1,2,4,2,6,3312]{5,3,4,2,1,0:T(2,128)} reshape(f32[2,4,2,6,2,2,6,138]{7,6,5,4,2,3,1,0:T(8,128)S(1)} %copy.44) | data formatting | bytes 2543616 | tf_op jit(solution)/shard_map/convert_element_type | solution.py:501
  192.4 76.9 %all-reduce.7.cloned.1.call-done = (bf16[1,192,2560]{2,1,0:T(8,128)(2,1)}, bf16[1,192,2560]{2,1,0:T(8,128)(2,1)}) async-done(((bf16[1,192,2560]{2,1,0:T(8,128)(2,1)}, bf16[1,192,2560]{2,1,0:T(8,128)(2,1)}), (bf16[1,192,2560]{2,1,0:T(8,128)(2,1)}, bf16[1,192,2560]{2,1,0:T(8,128)(2,1)})) %all-reduce.7.cloned.1.call-update) | async-done | bytes 1966096 | tf_op jit(solution)/shard_map/psum | solution.py:483
  269.3 2.0 convert_multiply_fusion
  (143 shorter events, 43.4 us)
Async XLA Ops:
  7.2 159.0 %all-reduce.5.cloned.1.call-start = ((), (), s32[]{:S(2)}) async-start(), calls=%async_computation | async-start | bytes 983040 | tf_op jit(solution)/shard_map/psum | solution.py:485
  15.5 10.8 %copy-start.5 = (bf16[192,768]{1,0:T(8,128)(2,1)}, bf16[192,768]{1,0:T(8,128)(2,1)S(1)}, u32[]{:S(2)}) copy-start(bf16[192,768]{1,0:T(8,128)(2,1)S(1)} %get-tuple-element.105.we) | copy-start | bytes 884740
  43.9 14.2 %collective-permute-start.2 = (bf16[144,192]{1,0:T(8,128)(2,1)S(1)}, bf16[144,192]{1,0:T(8,128)(2,1)S(1)}, u32[]{:S(2)}, u32[]{:S(2)}) collective-permute-start(bf16[144,192]{1,0:T(8,128)(2,1)S(1)} %get-tuple-element.121), channel_id=1, source_target_pairs={{0,7},{1,6},{2,1},{3,0},{4,3},{5,2},{6,5},{7,4},{8,15},{9,14},{10,... | collective-permute-start | bytes 165896 | tf_op jit(solution)/shard_map/ppermute | solution.py:401
  50.0 8.2 %collective-permute-start.1 = (bf16[144,192]{1,0:T(8,128)(2,1)S(1)}, bf16[144,192]{1,0:T(8,128)(2,1)S(1)}, u32[]{:S(2)}, u32[]{:S(2)}) collective-permute-start(bf16[144,192]{1,0:T(8,128)(2,1)S(1)} %get-tuple-element.122), channel_id=1, source_target_pairs={{0,1},{1,0},{2,3},{3,2},{4,5},{5,4},{6,7},{7,6},{8,9},{9,8},{10,11... | collective-permute-start | bytes 165896 | tf_op jit(solution)/shard_map/ppermute | solution.py:401
  50.5 7.7 %collective-permute-start = (bf16[144,192]{1,0:T(8,128)(2,1)S(1)}, bf16[144,192]{1,0:T(8,128)(2,1)S(1)}, u32[]{:S(2)}, u32[]{:S(2)}) collective-permute-start(bf16[144,192]{1,0:T(8,128)(2,1)S(1)} %get-tuple-element.123), channel_id=1, source_target_pairs={{0,6},{1,7},{2,0},{3,1},{4,2},{5,3},{6,4},{7,5},{8,14},{9,15},{10,... | collective-permute-start | bytes 165896 | tf_op jit(solution)/shard_map/ppermute | solution.py:401
  58.3 14.6 %copy-start.42 = (bf16[1,8,6,12,192]{4,1,3,2,0:T(8,128)(2,1)S(1)}, bf16[1,8,6,12,192]{4,1,3,2,0:T(8,128)(2,1)}, u32[]{:S(2)}) copy-start(bf16[1,8,6,12,192]{4,1,3,2,0:T(8,128)(2,1)} %param.14) | copy-start | bytes 663556
  68.9 11.1 %copy-start.10 = (bf16[576,576]{1,0:T(8,128)(2,1)S(1)}, bf16[576,576]{1,0:T(8,128)(2,1)}, u32[]{:S(2)}) copy-start(bf16[576,576]{1,0:T(8,128)(2,1)} %constant.25.clone.split) | copy-start | bytes 1990660
  68.9 11.1 %copy-start.12 = (bf16[192,768]{1,0:T(8,128)(2,1)S(1)}, bf16[192,768]{1,0:T(8,128)(2,1)}, u32[]{:S(2)}) copy-start(bf16[192,768]{1,0:T(8,128)(2,1)} %get-tuple-element.104.we) | copy-start | bytes 884740
  69.8 7.8 %collective-permute-start.5 = (bf16[144,192]{1,0:T(8,128)(2,1)}, bf16[144,192]{1,0:T(8,128)(2,1)S(1)}, u32[]{:S(2)}, u32[]{:S(2)}) collective-permute-start(bf16[144,192]{1,0:T(8,128)(2,1)} %get-tuple-element.117), channel_id=1, source_target_pairs={{0,3},{1,2},{2,5},{3,4},{4,7},{5,6},{6,1},{7,0},{8,11},{9,10},{10,... | collective-permute-start | bytes 165896 | tf_op jit(solution)/shard_map/ppermute | solution.py:401
  72.3 5.5 %collective-permute-start.4 = (bf16[144,192]{1,0:T(8,128)(2,1)}, bf16[144,192]{1,0:T(8,128)(2,1)}, u32[]{:S(2)}, u32[]{:S(2)}) collective-permute-start(bf16[144,192]{1,0:T(8,128)(2,1)} %get-tuple-element.118), channel_id=1, source_target_pairs={{0,1},{1,0},{2,3},{3,2},{4,5},{5,4},{6,7},{7,6},{8,9},{9,8},{10,11... | collective-permute-start | bytes 165896 | tf_op jit(solution)/shard_map/ppermute | solution.py:401
  72.8 6.3 %collective-permute-start.3 = (bf16[144,192]{1,0:T(8,128)(2,1)S(1)}, bf16[144,192]{1,0:T(8,128)(2,1)}, u32[]{:S(2)}, u32[]{:S(2)}) collective-permute-start(bf16[144,192]{1,0:T(8,128)(2,1)S(1)} %get-tuple-element.119), channel_id=1, source_target_pairs={{0,2},{1,3},{2,4},{3,5},{4,6},{5,7},{6,0},{7,1},{8,10},{9,11},{10,... | collective-permute-start | bytes 165896 | tf_op jit(solution)/shard_map/ppermute | solution.py:401
  82.0 11.7 %copy-start.32 = (bf16[576,192]{1,0:T(8,128)(2,1)S(1)}, bf16[576,192]{1,0:T(8,128)(2,1)}, u32[]{:S(2)}) copy-start(bf16[576,192]{1,0:T(8,128)(2,1)} %copy-done.31) | copy-start | bytes 663556
  82.0 11.7 %copy-start.34 = (bf16[576,192]{1,0:T(8,128)(2,1)S(1)}, bf16[576,192]{1,0:T(8,128)(2,1)}, u32[]{:S(2)}) copy-start(bf16[576,192]{1,0:T(8,128)(2,1)} %copy-done.33) | copy-start | bytes 663556
  82.0 11.7 %copy-start.36 = (bf16[576,192]{1,0:T(8,128)(2,1)S(1)}, bf16[576,192]{1,0:T(8,128)(2,1)}, u32[]{:S(2)}) copy-start(bf16[576,192]{1,0:T(8,128)(2,1)} %copy-done.35) | copy-start | bytes 663556
  82.0 11.8 %copy-start.38 = (bf16[576,192]{1,0:T(8,128)(2,1)S(1)}, bf16[576,192]{1,0:T(8,128)(2,1)}, u32[]{:S(2)}) copy-start(bf16[576,192]{1,0:T(8,128)(2,1)} %copy-done.37) | copy-start | bytes 663556
  82.0 11.8 %copy-start.40 = (bf16[576,192]{1,0:T(8,128)(2,1)S(1)}, bf16[576,192]{1,0:T(8,128)(2,1)}, u32[]{:S(2)}) copy-start(bf16[576,192]{1,0:T(8,128)(2,1)} %copy-done.39) | copy-start | bytes 663556
  87.3 5.3 %collective-permute-start.8 = (bf16[144,192]{1,0:T(8,128)(2,1)S(1)}, bf16[144,192]{1,0:T(8,128)(2,1)S(1)}, u32[]{:S(2)}, u32[]{:S(2)}) collective-permute-start(bf16[144,192]{1,0:T(8,128)(2,1)S(1)} %get-tuple-element.113), channel_id=1, source_target_pairs={{0,7},{1,6},{2,1},{3,0},{4,3},{5,2},{6,5},{7,4},{8,15},{9,14},{10,... | collective-permute-start | bytes 165896 | tf_op jit(solution)/shard_map/ppermute | solution.py:401
  88.8 4.6 %collective-permute-start.7 = (bf16[144,192]{1,0:T(8,128)(2,1)S(1)}, bf16[144,192]{1,0:T(8,128)(2,1)S(1)}, u32[]{:S(2)}, u32[]{:S(2)}) collective-permute-start(bf16[144,192]{1,0:T(8,128)(2,1)S(1)} %get-tuple-element.114), channel_id=1, source_target_pairs={{0,1},{1,0},{2,3},{3,2},{4,5},{5,4},{6,7},{7,6},{8,9},{9,8},{10,11... | collective-permute-start | bytes 165896 | tf_op jit(solution)/shard_map/ppermute | solution.py:401
  89.3 4.4 %collective-permute-start.6 = (bf16[144,192]{1,0:T(8,128)(2,1)S(1)}, bf16[144,192]{1,0:T(8,128)(2,1)S(1)}, u32[]{:S(2)}, u32[]{:S(2)}) collective-permute-start(bf16[144,192]{1,0:T(8,128)(2,1)S(1)} %get-tuple-element.115), channel_id=1, source_target_pairs={{0,6},{1,7},{2,0},{3,1},{4,2},{5,3},{6,4},{7,5},{8,14},{9,15},{10,... | collective-permute-start | bytes 165896 | tf_op jit(solution)/shard_map/ppermute | solution.py:401
  103.1 10.1 %collective-permute-start.11 = (bf16[144,192]{1,0:T(8,128)(2,1)S(1)}, bf16[144,192]{1,0:T(8,128)(2,1)S(1)}, u32[]{:S(2)}, u32[]{:S(2)}) collective-permute-start(bf16[144,192]{1,0:T(8,128)(2,1)S(1)} %get-tuple-element.109), channel_id=1, source_target_pairs={{0,3},{1,2},{2,5},{3,4},{4,7},{5,6},{6,1},{7,0},{8,11},{9,10},{10,... | collective-permute-start | bytes 165896 | tf_op jit(solution)/shard_map/ppermute | solution.py:401
  105.7 7.5 %collective-permute-start.10 = (bf16[144,192]{1,0:T(8,128)(2,1)S(1)}, bf16[144,192]{1,0:T(8,128)(2,1)S(1)}, u32[]{:S(2)}, u32[]{:S(2)}) collective-permute-start(bf16[144,192]{1,0:T(8,128)(2,1)S(1)} %get-tuple-element.110), channel_id=1, source_target_pairs={{0,1},{1,0},{2,3},{3,2},{4,5},{5,4},{6,7},{7,6},{8,9},{9,8},{10,11... | collective-permute-start | bytes 165896 | tf_op jit(solution)/shard_map/ppermute | solution.py:401
  106.2 7.0 %collective-permute-start.9 = (bf16[144,192]{1,0:T(8,128)(2,1)S(1)}, bf16[144,192]{1,0:T(8,128)(2,1)S(1)}, u32[]{:S(2)}, u32[]{:S(2)}) collective-permute-start(bf16[144,192]{1,0:T(8,128)(2,1)S(1)} %get-tuple-element.111), channel_id=1, source_target_pairs={{0,2},{1,3},{2,4},{3,5},{4,6},{5,7},{6,0},{7,1},{8,10},{9,11},{10,... | collective-permute-start | bytes 165896 | tf_op jit(solution)/shard_map/ppermute | solution.py:401
  126.8 142.4 %all-reduce.7.cloned.1.call-start = ((), (), s32[]{:S(2)}) async-start(), calls=%async_computation.1 | async-start | bytes 3932160 | tf_op jit(solution)/shard_map/psum | solution.py:483
  127.6 3.5 %collective-permute-start.12 = (bf16[576,192]{1,0:T(8,128)(2,1)S(1)}, bf16[576,192]{1,0:T(8,128)(2,1)S(1)}, u32[]{:S(2)}, u32[]{:S(2)}) collective-permute-start(bf16[576,192]{1,0:T(8,128)(2,1)S(1)} %get-tuple-element.65), channel_id=1, source_target_pairs={{8,0},{16,8},{24,16},{9,1},{17,9},{25,17},{10,2},{18,10},{26,18},{... | collective-permute-start | bytes 663560 | tf_op jit(solution)/shard_map/ppermute | solution.py:477
  (34 other events, 107.5 us)
Sparse Core Ops, SparseCore 0:
  127.0 39.2 all-reduce.4
  170.8 98.4 all-reduce.6

commit v2 on v1

--- a/solution.py
+++ b/solution.py
@@ -407,12 +407,6 @@
     )
 
 
-def reduce_all(grads, table):
-    total = lax.psum(grads, ("lon", "lat"))
-    table = lax.psum(table, "lon")
-    return total, lax.all_gather(table, "lat", axis=0)
-
-
 def on_device(
     inputs, grad_output, norm_gains, input_weight, output_weight, expand_weight, reduce_weight,
     bias_table,
@@ -473,17 +467,219 @@
         (bf(D, GRAD_LANES), tok, bf(TABLE_PAD, PAIRS_PAD)),
         (tok, wide, ff(TOKENS, D), tok, tok, tok, tok, tok, *half_bias, ff(32, PAIRS_PAD)),
     )
+    upstream, sum0, sum1, tables = reduce_grads(g0, g1, t0, t1, e0)
+    return finish(upstream, sum0, sum1, tables, lat_total, inputs.shape)
+
+
+def reduce_grads(g0, g1, t0, t1, e0):
+    if lax.axis_size("lon") == 4 and lax.axis_size("lat") == 2:
+        return reduce_by_kernel(g0, g1, t0, t1, e0)
     sections = lax.axis_size("section")
     upstream = lax.ppermute(e0, "section", [(i, i - 1) for i in range(1, sections)])
-    sum1, sum0, tables = reduce_grads(g0, g1, t0, t1)
-    return finish(upstream, sum0, sum1, tables, lat_total, inputs.shape)
-
-
-def reduce_grads(g0, g1, t0, t1):
     sum1 = lax.psum(g1, ("lon", "lat"))
     sum0 = lax.psum(g0, ("lon", "lat"))
     tables = lax.all_gather(lax.psum(jnp.stack([t0, t1]), "lon"), "lat", axis=0)
-    return sum1, sum0, tables
+    return upstream, sum0, sum1, tables
+
+
+PACKETS = (
+    (1024, 768, "yab"),
+    (0, 512, "aby"),
+    (1792, 768, "yab"),
+    (512, 512, "aby"),
+)
+
+
+def halved(shape, dim):
+    rows, lanes = shape
+    return (rows, lanes // 2) if dim == "y" else (rows // 2, lanes)
+
+
+def packet_shapes(shape, order):
+    shapes = []
+    for dim in order:
+        shape = halved(shape, dim)
+        shapes.append(shape)
+    return shapes
+
+
+class Packet:
+    def __init__(self, src, out, lane0, width, order, bits, peers, bufs, send, recv):
+        self.src, self.out, self.order = src, out, order
+        self.bits, self.peers, self.bufs = bits, peers, bufs
+        self.send, self.recv = send, recv
+        self.row, self.lane = 0, lane0
+        self.shape = (src.shape[0], width)
+        self.local = (0, lane0)
+        self.held = src
+        self.copy = None
+        self.trail = []
+
+    def cut(self, dim, bit):
+        rows, lanes = halved(self.shape, dim)
+        if dim == "y":
+            return 0, pl.multiple_of(bit * lanes, 128), rows, lanes
+        return pl.multiple_of(bit * rows, 16), 0, rows, lanes
+
+    def start(self, k):
+        dim = self.order[k]
+        dr, dl, rows, lanes = self.cut(dim, 1 - self.bits[dim])
+        self.copy = pltpu.make_async_remote_copy(
+            src_ref=self.held.at[at(self.local[0], dr, rows, 16), at(self.local[1], dl, lanes, 128)],
+            dst_ref=self.bufs[2 * k],
+            send_sem=self.send.at[k],
+            recv_sem=self.recv.at[k],
+            device_id=self.peers[dim],
+            device_id_type=pl.DeviceIdType.MESH,
+        )
+        self.copy.start()
+
+    def add(self, k):
+        self.copy.wait()
+        dim = self.order[k]
+        dr, dl, rows, lanes = self.cut(dim, self.bits[dim])
+        mine = self.held[at(self.local[0], dr, rows, 16), at(self.local[1], dl, lanes, 128)]
+        total = mine + self.bufs[2 * k][...]
+        self.trail.append((self.row, self.lane, self.shape))
+        self.row, self.lane, self.shape = self.row + dr, self.lane + dl, (rows, lanes)
+        if k == len(self.order) - 1:
+            self.out[at(self.row, 0, rows, 16), at(self.lane, 0, lanes, 128)] = total
+        else:
+            self.held = self.bufs[2 * k + 1]
+            self.held[...] = total
+            self.local = (0, 0)
+
+    def start_back(self, k):
+        dim = self.order[k]
+        n = len(self.order)
+        rows, lanes = self.shape
+        part = self.out.at[at(self.row, 0, rows, 16), at(self.lane, 0, lanes, 128)]
+        self.copy = pltpu.make_async_remote_copy(
+            src_ref=part,
+            dst_ref=part,
+            send_sem=self.send.at[n + k],
+            recv_sem=self.recv.at[n + k],
+            device_id=self.peers[dim],
+            device_id_type=pl.DeviceIdType.MESH,
+        )
+        self.copy.start()
+
+    def finish_back(self):
+        self.copy.wait()
+        self.row, self.lane, self.shape = self.trail.pop()
+
+
+def at(base, offset, size, unit):
+    start = base + offset
+    if isinstance(start, int):
+        return pl.ds(start, size)
+    return pl.ds(pl.multiple_of(start, unit), size)
+
+
+def reduce_kernel(g0, g1, t0, t1, e0, r0, r1, tt, eo, *scratch):
+    *bufs, send, recv = scratch
+    lat, lon = lax.axis_index("lat"), lax.axis_index("lon")
+    sec, sections = lax.axis_index("section"), lax.axis_size("section")
+    low, high = lax.rem(lon, 2), lax.div(lon, 2)
+    bits = {"y": lat, "a": low, "b": high}
+    here = {"section": sec, "lon": lon, "lat": lat}
+    peers = {
+        "y": {**here, "lat": 1 - lat},
+        "a": {**here, "lon": lon + 1 - 2 * low},
+        "b": {**here, "lon": lon + 2 - 4 * high},
+    }
+    before = {**here, "section": lax.rem(sec + sections - 1, sections)}
+    after = {**here, "section": lax.rem(sec + 1, sections)}
+    barrier = pltpu.get_barrier_semaphore()
+    for peer in (*peers.values(), before, after):
+        pl.semaphore_signal(
+            barrier, inc=1, device_id=peer, device_id_type=pl.DeviceIdType.MESH
+        )
+    pl.semaphore_wait(barrier, 5)
+
+    packets = []
+    used = 0
+    for src, out in ((g1, r1), (g0, r0)):
+        for lane0, width, order in PACKETS:
+            i = len(packets)
+            packets.append(
+                Packet(src, out, lane0, width, order, bits, peers,
+                       bufs[used : used + 5], send.at[i], recv.at[i])
+            )
+            used += 5
+    tables = []
+    for b, src in ((1, t1), (0, t0)):
+        i = len(packets) + len(tables)
+        tables.append(
+            Packet(src, tt.at[lat, b], 0, PAIRS_PAD, "ab", bits, peers,
+                   bufs[used : used + 3], send.at[i], recv.at[i])
+        )
+        used += 3
+    for p in packets[:4] + tables[:1] + packets[4:] + tables[1:]:
+        p.start(0)
+    i = len(packets) + len(tables)
+    up = pltpu.make_async_remote_copy(
+        src_ref=e0, dst_ref=eo, send_sem=send.at[i, 0], recv_sem=recv.at[i, 0],
+        device_id=before, device_id_type=pl.DeviceIdType.MESH,
+    )
+    up.start()
+    flow = packets[:4] + tables[:1] + packets[4:] + tables[1:]
+    for k in range(3):
+        for p in flow:
+            n = len(p.order)
+            if k < n:
+                p.add(k)
+                if k + 1 < n:
+                    p.start(k + 1)
+                else:
+                    p.start_back(n - 1)
+            else:
+                p.finish_back()
+                p.start_back(0)
+    for k in range(3):
+        for p in flow:
+            n = len(p.order)
+            if n == 3:
+                p.finish_back()
+                if k < 2:
+                    p.start_back(1 - k)
+            elif k == 0:
+                p.finish_back()
+                i = 4
+                p.copy = pltpu.make_async_remote_copy(
+                    src_ref=p.out, dst_ref=p.out, send_sem=p.send.at[i], recv_sem=p.recv.at[i],
+                    device_id=peers["y"], device_id_type=pl.DeviceIdType.MESH,
+                )
+                p.copy.start()
+            elif k == 2:
+                p.copy.wait()
+    up.wait()
+
+
+def reduce_by_kernel(g0, g1, t0, t1, e0):
+    scratch = []
+    for _ in range(2):
+        for _, width, order in PACKETS:
+            one, two, three = packet_shapes((D, width), order)
+            scratch += [one, one, two, two, three]
+    for _ in range(2):
+        one, two = packet_shapes((TABLE_PAD, PAIRS_PAD), "ab")
+        scratch += [one, one, two]
+    count = 2 * len(PACKETS) + 3
+    outs = (bf(D, GRAD_LANES), bf(D, GRAD_LANES), bf(2, 2, TABLE_PAD, PAIRS_PAD), bf(TOKENS, D))
+    r0, r1, tt, eo = pl.pallas_call(
+        reduce_kernel,
+        out_shape=outs,
+        in_specs=[pl.BlockSpec(memory_space=pltpu.VMEM)] * 5,
+        out_specs=tuple(pl.BlockSpec(memory_space=pltpu.VMEM) for _ in outs),
+        scratch_shapes=[pltpu.VMEM(s, BF16) for s in scratch]
+        + [pltpu.SemaphoreType.DMA((count, 6)), pltpu.SemaphoreType.DMA((count, 6))],
+        compiler_params=pltpu.CompilerParams(
+            collective_id=0, has_side_effects=True, vmem_limit_bytes=VMEM_BYTES
+        ),
+    )(g0, g1, t0, t1, e0)
+    last = lax.axis_index("section") == lax.axis_size("section") - 1
+    return jnp.where(last, jnp.zeros_like(eo), eo), r0, r1, tt
 
 
 def finish(upstream, sum0, sum1, tables, lat_total, shape):

time: 282 us -> 222 us (0.79)
  waiting for transfers between devices: 122 us -> 9.32 us
  Pallas kernels: 57.4 us -> 134 us
  blocking collectives: 16.2 us -> 0 us
  between operations: 14.5 us -> 1.1 us
  local copies, waits for them, and re-layouts: 49.2 us -> 57.7 us
    psum x2 -> x0, waiting for transfers between devices: 111 us -> none  [the longest x1 76.9 us: reduce_grads(): sum1 = lax.psum(g1, ('lon', 'lat'))]
    pallas_call x0 -> x1, Pallas kernels: none -> 76.3 us  [reduce_by_kernel(): pl.pallas_call(reduce_kernel, out_shape=outs, in_specs=[pl.BlockSpec(memo...]
    all_gather x1 -> x0, blocking collectives: 16.2 us -> none  [reduce_grads(): tables = lax.all_gather(lax.psum(jnp.stack([t0, t1]), 'lon'), 'lat', axis=0)]
    unnamed x92 -> x102, local copies, waits for them, and re-layouts: 18.8 us -> 26.1 us
  transfers between devices with their start and end apart: 15 -> 12, of which waited for: 9 -> 6; matrix products, arithmetic and copies ran while one was open for 5% -> 0% of each run, Pallas kernels for 3% -> 4%
where the time goes in v2:
time: 222 us; the launch traced here: 220 us
  Pallas kernels  134 us (60%)
  local copies, waits for them, and re-layouts  57.7 us (26%)
  starting transfers between devices  15.4 us (7%)
  waiting for transfers between devices  9.32 us (4%)
  other arithmetic  2.92 us (1%)
    pallas_call x1, Pallas kernels, reduce_by_kernel(): pl.pallas_call(reduce_kernel, out_shape=outs, in_specs=[pl.BlockSpec(memo...  76.3 us
    pallas_call x7, Pallas kernels, run(): pl.pallas_call(body, out_shape=tuple(outs), in_specs=[pl.BlockSpec(memory...  57.3 us
    unnamed x102, local copies, waits for them, and re-layouts  26.1 us
    ppermute x12, starting transfers between devices, moved(): return lax.ppermute(part, ('lon', 'lat'), pairs)  15.4 us
    convert_element_type x3, local copies, waits for them, and re-layouts, finish(): tab = tab.reshape(1, 2, LEVEL_WINDOWS, lat_n, HEADS, SLOTS).astype(F32)  11.9 us
    ppermute x12, waiting for transfers between devices, moved(): return lax.ppermute(part, ('lon', 'lat'), pairs)  9.32 us
  transfers between devices with their start and end apart: 12, of which 6 were waited for; matrix products, arithmetic and copies ran while one was open for 0% of the time, Pallas kernels for 4%

profile of v2, /device:TPU:0, one launch (start us, length us, event | category | flops | bytes accessed | tf_op | source)
XLA Modules:
  0.0 220.0 jit_solution(6144570003732407272)
XLA Ops:
  4.2 1.9 slice_bitcast_fusion.5
  9.1 2.9 %reshape_squeeze.7 = f32[2,24,2,2,6,138]{5,4,3,2,0,1:T(8,128)} reshape(f32[1,2,4,1,6,3312]{5,1,4,2,3,0:T(2,128)S(1)} %copy.30) | data formatting | bytes 1271808 | tf_op jit(solution)/shard_map/reshape;squeeze | solution.py:426
  11.9 2.0 copy.31
  13.9 1.9 reshape.77
  15.9 2.0 fusion.1
  17.9 13.3 %shard_map.180 = (bf16[576,192]{1,0:T(8,128)(2,1)S(1)}, bf16[576,192]{1,0:T(8,128)(2,1)S(1)}, bf16[576,192]{1,0:T(8,128)(2,1)S(1)}, bf16[576,192]{1,0:T(8,128)(2...) custom-call(bf16[576,192]{1,0:T(8,128)(2,1)S(1)} %reshape.75.x, ...), custom_call_target="tpu_custom_call" | custom-call | flops 1000000000 | bytes 10000000 | tf_op jit(solution)/shard_map/pallas_call | solution.py:381
  35.5 6.1 %collective-permute-start.2 = (bf16[144,192]{1,0:T(8,128)(2,1)S(1)}, bf16[144,192]{1,0:T(8,128)(2,1)S(1)}, u32[]{:S(2)}, u32[]{:S(2)}) collective-permute-start(bf16[144,192]{1,0:T(8,128)(2,1)S(1)} %get-tuple-element.120), channel_id=1, source_target_pairs={{0,7},{1,6},{2,1},{3,0},{4,3},{5,2},{6,5},{7,4},{8,15},{9,14},{10,... | collective-permute-start | bytes 165896 | tf_op jit(solution)/shard_map/ppermute | solution.py:401
  42.5 4.7 %shard_map.181 = (f32[3456,128]{1,0:T(8,128)S(1)}, f32[3456,128]{1,0:T(8,128)S(1)}) custom-call(f32[288,384]{1,0:T(8,128)S(1)} %get-tuple-element.99.table_ref, bf16[12,384,256]{2,1,0:T(8,128)(2,1)} %constant.38.clone.spread.spread_ref), custom_call_target="tpu_custom_call" | custom-call | flops 1000000000 | bytes 10000000 | tf_op jit(solution)/shard_map/pallas_call | solution.py:381
  49.8 8.4 %shard_map.182 = (bf16[576,192]{1,0:T(8,128)(2,1)S(1)}, bf16[576,192]{1,0:T(8,128)(2,1)S(1)}, bf16[576,192]{1,0:T(8,128)(2,1)S(1)}, bf16[576,192]{1,0:T(8,128)(2...) custom-call(bf16[576,192]{1,0:T(8,128)(2,1)S(1)} %pad_maximum_fusion.rq, ...), custom_call_target="tpu_custom_call" | custom-call | flops 1000000000 | bytes 10000000 | tf_op jit(solution)/shard_map/pallas_call | solution.py:381
  61.3 2.5 %collective-permute-start.5 = (bf16[144,192]{1,0:T(8,128)(2,1)}, bf16[144,192]{1,0:T(8,128)(2,1)S(1)}, u32[]{:S(2)}, u32[]{:S(2)}) collective-permute-start(bf16[144,192]{1,0:T(8,128)(2,1)} %get-tuple-element.116), channel_id=1, source_target_pairs={{0,3},{1,2},{2,5},{3,4},{4,7},{5,6},{6,1},{7,0},{8,11},{9,10},{10,... | collective-permute-start | bytes 165896 | tf_op jit(solution)/shard_map/ppermute | solution.py:401
  65.5 3.6 %collective-permute-done.5 = bf16[144,192]{1,0:T(8,128)(2,1)S(1)} collective-permute-done((bf16[144,192]{1,0:T(8,128)(2,1)}, bf16[144,192]{1,0:T(8,128)(2,1)S(1)}, u32[]{:S(2)}, u32[]{:S(2)}) %collective-permute-start.5) | collective-permute-done | bytes 55328 | tf_op jit(solution)/shard_map/ppermute | solution.py:401
  74.4 5.2 %shard_map.183 = (f32[576,192]{1,0:T(8,128)S(1)}, bf16[192,1536]{1,0:T(8,128)(2,1)S(1)}, f32[8,192]{1,0:T(8,128)S(1)}, bf16[576,192]{1,0:T(8,128)(2,1)S(1)}) custom-call(bf16[576,192]{1,0:T(8,128)(2,1)S(1)} %pad_maximum_fusion.1.rq, bf16[576,192]{1,0:T(8,128)(2,1)S(1)} %copy-done.31, bf16[576,192]{1,0:T(8,128)(2,1)S(1)} %copy-done.15, ...), custom_call_target="tpu_custom_call" | custom-call | flops 1000000000 | bytes 10000000 | tf_op jit(solution)/shard_map/pallas_call | solution.py:381
  83.3 3.2 %collective-permute-done.8 = bf16[144,192]{1,0:T(8,128)(2,1)S(1)} collective-permute-done((bf16[144,192]{1,0:T(8,128)(2,1)S(1)}, bf16[144,192]{1,0:T(8,128)(2,1)S(1)}, u32[]{:S(2)}, u32[]{:S(2)}) %collective-permute-start.8) | collective-permute-done | bytes 55328 | tf_op jit(solution)/shard_map/ppermute | solution.py:401
  93.5 9.3 %shard_map.184 = (bf16[192,2560]{1,0:T(8,128)(2,1)}, bf16[576,192]{1,0:T(8,128)(2,1)S(1)}, f32[3456,128]{1,0:T(8,128)}, f32[3456,128]{1,0:T(8,128)}) custom-call(bf16[576,192]{1,0:T(8,128)(2,1)S(1)} %pad_maximum_fusion.2.rq, bf16[192,1536]{1,0:T(8,128)(2,1)S(1)} %copy-done.13, bf16[576,192]{1,0:T(8,128)(2,1)S(1)} %copy-done.34, ...), custom_call_target="tpu_custom_call" | custom-call | flops 1000000000 | bytes 10000000 | tf_op jit(solution)/shard_map/pallas_call | solution.py:381
  102.8 2.6 %collective-permute-start.11 = (bf16[144,192]{1,0:T(8,128)(2,1)S(1)}, bf16[144,192]{1,0:T(8,128)(2,1)S(1)}, u32[]{:S(2)}, u32[]{:S(2)}) collective-permute-start(bf16[144,192]{1,0:T(8,128)(2,1)S(1)} %get-tuple-element.108), channel_id=1, source_target_pairs={{0,3},{1,2},{2,5},{3,4},{4,7},{5,6},{6,1},{7,0},{8,11},{9,10},{10,... | collective-permute-start | bytes 165896 | tf_op jit(solution)/shard_map/ppermute | solution.py:401
  106.0 1.5 copy-done.6
  107.5 1.5 copy-done.7
  109.0 3.8 %shard_map.186.t1 = bf16[320,384]{1,0:T(8,128)(2,1)S(1)} custom-call(f32[3456,128]{1,0:T(8,128)S(1)} %copy-done.6, f32[3456,128]{1,0:T(8,128)S(1)} %copy-done.7, bf16[12,384,256]{2,1,0:T(8,128)(2,1)} %constant.38.clone.spread.spread_ref), custom_call_target="tpu_custom_call" | custom-call | flops 1000000000 | bytes 10000000 | tf_op jit(solution)/shard_map/pallas_call | solution.py:381
  113.0 12.6 %shard_map.185 = (bf16[192,2560]{1,0:T(8,128)(2,1)}, bf16[576,192]{1,0:T(8,128)(2,1)S(1)}, bf16[320,384]{1,0:T(8,128)(2,1)S(1)}) custom-call(bf16[576,192]{1,0:T(8,128)(2,1)S(1)} %pad_maximum_fusion.3.rq, f32[576,192]{1,0:T(8,128)} %copy-done.11, bf16[576,192]{1,0:T(8,128)(2,1)S(1)} %copy-done.32, bf16[576,192]{1,0:T(8,128)(2,1)S(1)} %reshape.75.x, ...), custom_call_target="tpu_custom_call" | custom-call | flops 1000000000 | bytes 10000000 | tf_op jit(solution)/shard_map/pallas_call | solution.py:381
  125.7 76.3 %shard_map.187 = (bf16[192,2560]{1,0:T(8,128)(2,1)S(1)}, bf16[192,2560]{1,0:T(8,128)(2,1)S(1)}, bf16[2,2,320,384]{3,2,1,0:T(8,128)(2,1)S(1)}, bf16[576,192]{1,0:T(8,128)(2,1)S(1)}) custom-call(bf16[192,2560]{1,0:T(8,128)(2,1)} %get-tuple-element.69.g0, bf16[192,2560]{1,0:T(8,128)(2,1)} %get-tuple-element.70.g1, bf16[320,384]{1,0:T(8,128)(2,1)S(1)} %get-tuple-element.71.t0, ...), custom_call_target="tpu_custom_call" | custom-call | tf_op jit(solution)/shard_map/pallas_call | solution.py:670
  203.6 1.6 slice_bitcast_fusion
  206.9 3.5 %reshape.81 = f32[2,2,4,6,2,6,2,138]{7,6,5,4,3,2,1,0:T(2,128)} reshape(f32[2,2,288,276]{3,2,1,0:T(8,128)S(1)} %slice_convert_fusion) | data formatting | bytes 2543616 | tf_op jit(solution)/shard_map/convert_element_type | solution.py:697
  210.3 3.8 %copy.34 = f32[2,4,2,6,2,2,6,138]{7,6,5,4,2,3,1,0:T(8,128)} copy(f32[2,4,2,6,2,2,6,138]{7,5,6,4,3,1,0,2:T(2,128)} %bitcast.45) | data formatting | bytes 2543616 | tf_op jit(solution)/shard_map/convert_element_type | solution.py:697
  214.2 4.6 %reshape.80 = f32[1,2,4,2,6,3312]{5,3,4,2,1,0:T(2,128)} reshape(f32[2,4,2,6,2,2,6,138]{7,6,5,4,2,3,1,0:T(8,128)} %copy.34) | data formatting | bytes 2543616 | tf_op jit(solution)/shard_map/convert_element_type | solution.py:697
  (145 shorter events, 40.2 us)
Async XLA Ops:
  0.6 7.4 %copy-start = (f32[1,2,4,2,6,3312]{5,3,4,2,1,0:T(2,128)S(1)}, f32[1,2,4,2,6,3312]{5,3,4,2,1,0:T(2,128)}, u32[]{:S(2)}) copy-start(f32[1,2,4,2,6,3312]{5,3,4,2,1,0:T(2,128)} %param.20) | copy-start | bytes 3815428
  6.1 11.8 %copy-start.5 = (bf16[192,768]{1,0:T(8,128)(2,1)}, bf16[192,768]{1,0:T(8,128)(2,1)S(1)}, u32[]{:S(2)}) copy-start(bf16[192,768]{1,0:T(8,128)(2,1)S(1)} %get-tuple-element.104.we) | copy-start | bytes 884740
  8.0 9.8 %copy-start.2 = (bf16[1,1,768,192]{3,2,1,0:T(8,128)(2,1)}, bf16[1,1,768,192]{3,2,1,0:T(8,128)(2,1)S(1)}, u32[]{:S(2)}) copy-start(bf16[1,1,768,192]{3,2,1,0:T(8,128)(2,1)S(1)} %copy.36) | copy-start | bytes 884740
  35.5 7.0 %copy-start.16 = (bf16[576,192]{1,0:T(8,128)(2,1)}, bf16[576,192]{1,0:T(8,128)(2,1)S(1)}, u32[]{:S(2)}) copy-start(bf16[576,192]{1,0:T(8,128)(2,1)S(1)} %get-tuple-element.59.fr) | copy-start | bytes 663556
  35.5 7.0 %copy-start.18 = (bf16[576,192]{1,0:T(8,128)(2,1)}, bf16[576,192]{1,0:T(8,128)(2,1)S(1)}, u32[]{:S(2)}) copy-start(bf16[576,192]{1,0:T(8,128)(2,1)S(1)} %get-tuple-element.60.q) | copy-start | bytes 663556
  35.5 14.2 %collective-permute-start.2 = (bf16[144,192]{1,0:T(8,128)(2,1)S(1)}, bf16[144,192]{1,0:T(8,128)(2,1)S(1)}, u32[]{:S(2)}, u32[]{:S(2)}) collective-permute-start(bf16[144,192]{1,0:T(8,128)(2,1)S(1)} %get-tuple-element.120), channel_id=1, source_target_pairs={{0,7},{1,6},{2,1},{3,0},{4,3},{5,2},{6,5},{7,4},{8,15},{9,14},{10,... | collective-permute-start | bytes 165896 | tf_op jit(solution)/shard_map/ppermute | solution.py:401
  41.5 8.2 %collective-permute-start.1 = (bf16[144,192]{1,0:T(8,128)(2,1)S(1)}, bf16[144,192]{1,0:T(8,128)(2,1)S(1)}, u32[]{:S(2)}, u32[]{:S(2)}) collective-permute-start(bf16[144,192]{1,0:T(8,128)(2,1)S(1)} %get-tuple-element.121), channel_id=1, source_target_pairs={{0,1},{1,0},{2,3},{3,2},{4,5},{5,4},{6,7},{7,6},{8,9},{9,8},{10,11... | collective-permute-start | bytes 165896 | tf_op jit(solution)/shard_map/ppermute | solution.py:401
  42.0 7.7 %collective-permute-start = (bf16[144,192]{1,0:T(8,128)(2,1)S(1)}, bf16[144,192]{1,0:T(8,128)(2,1)S(1)}, u32[]{:S(2)}, u32[]{:S(2)}) collective-permute-start(bf16[144,192]{1,0:T(8,128)(2,1)S(1)} %get-tuple-element.122), channel_id=1, source_target_pairs={{0,6},{1,7},{2,0},{3,1},{4,2},{5,3},{6,4},{7,5},{8,14},{9,15},{10,... | collective-permute-start | bytes 165896 | tf_op jit(solution)/shard_map/ppermute | solution.py:401
  42.5 7.3 %copy-start.3 = (bf16[576,576]{1,0:T(8,128)(2,1)S(1)}, bf16[576,576]{1,0:T(8,128)(2,1)}, u32[]{:S(2)}) copy-start(bf16[576,576]{1,0:T(8,128)(2,1)} %constant.37.clone.join_t) | copy-start | bytes 1990660
  42.5 7.3 %copy-start.4 = (bf16[576,576]{1,0:T(8,128)(2,1)S(1)}, bf16[576,576]{1,0:T(8,128)(2,1)}, u32[]{:S(2)}) copy-start(bf16[576,576]{1,0:T(8,128)(2,1)} %constant.36.clone.join) | copy-start | bytes 1990660
  49.8 14.6 %copy-start.47 = (bf16[1,8,6,12,192]{4,1,3,2,0:T(8,128)(2,1)S(1)}, bf16[1,8,6,12,192]{4,1,3,2,0:T(8,128)(2,1)}, u32[]{:S(2)}) copy-start(bf16[1,8,6,12,192]{4,1,3,2,0:T(8,128)(2,1)} %param.14) | copy-start | bytes 663556
  60.4 11.1 %copy-start.10 = (bf16[576,576]{1,0:T(8,128)(2,1)S(1)}, bf16[576,576]{1,0:T(8,128)(2,1)}, u32[]{:S(2)}) copy-start(bf16[576,576]{1,0:T(8,128)(2,1)} %constant.34.clone.split) | copy-start | bytes 1990660
  61.3 7.8 %collective-permute-start.5 = (bf16[144,192]{1,0:T(8,128)(2,1)}, bf16[144,192]{1,0:T(8,128)(2,1)S(1)}, u32[]{:S(2)}, u32[]{:S(2)}) collective-permute-start(bf16[144,192]{1,0:T(8,128)(2,1)} %get-tuple-element.116), channel_id=1, source_target_pairs={{0,3},{1,2},{2,5},{3,4},{4,7},{5,6},{6,1},{7,0},{8,11},{9,10},{10,... | collective-permute-start | bytes 165896 | tf_op jit(solution)/shard_map/ppermute | solution.py:401
  63.8 5.5 %collective-permute-start.4 = (bf16[144,192]{1,0:T(8,128)(2,1)}, bf16[144,192]{1,0:T(8,128)(2,1)}, u32[]{:S(2)}, u32[]{:S(2)}) collective-permute-start(bf16[144,192]{1,0:T(8,128)(2,1)} %get-tuple-element.117), channel_id=1, source_target_pairs={{0,1},{1,0},{2,3},{3,2},{4,5},{5,4},{6,7},{7,6},{8,9},{9,8},{10,11... | collective-permute-start | bytes 165896 | tf_op jit(solution)/shard_map/ppermute | solution.py:401
  64.3 6.3 %collective-permute-start.3 = (bf16[144,192]{1,0:T(8,128)(2,1)S(1)}, bf16[144,192]{1,0:T(8,128)(2,1)}, u32[]{:S(2)}, u32[]{:S(2)}) collective-permute-start(bf16[144,192]{1,0:T(8,128)(2,1)S(1)} %get-tuple-element.118), channel_id=1, source_target_pairs={{0,2},{1,3},{2,4},{3,5},{4,6},{5,7},{6,0},{7,1},{8,10},{9,11},{10,... | collective-permute-start | bytes 165896 | tf_op jit(solution)/shard_map/ppermute | solution.py:401
  81.2 5.3 %collective-permute-start.8 = (bf16[144,192]{1,0:T(8,128)(2,1)S(1)}, bf16[144,192]{1,0:T(8,128)(2,1)S(1)}, u32[]{:S(2)}, u32[]{:S(2)}) collective-permute-start(bf16[144,192]{1,0:T(8,128)(2,1)S(1)} %get-tuple-element.112), channel_id=1, source_target_pairs={{0,7},{1,6},{2,1},{3,0},{4,3},{5,2},{6,5},{7,4},{8,15},{9,14},{10,... | collective-permute-start | bytes 165896 | tf_op jit(solution)/shard_map/ppermute | solution.py:401
  82.7 4.6 %collective-permute-start.7 = (bf16[144,192]{1,0:T(8,128)(2,1)S(1)}, bf16[144,192]{1,0:T(8,128)(2,1)S(1)}, u32[]{:S(2)}, u32[]{:S(2)}) collective-permute-start(bf16[144,192]{1,0:T(8,128)(2,1)S(1)} %get-tuple-element.113), channel_id=1, source_target_pairs={{0,1},{1,0},{2,3},{3,2},{4,5},{5,4},{6,7},{7,6},{8,9},{9,8},{10,11... | collective-permute-start | bytes 165896 | tf_op jit(solution)/shard_map/ppermute | solution.py:401
  83.2 4.4 %collective-permute-start.6 = (bf16[144,192]{1,0:T(8,128)(2,1)S(1)}, bf16[144,192]{1,0:T(8,128)(2,1)S(1)}, u32[]{:S(2)}, u32[]{:S(2)}) collective-permute-start(bf16[144,192]{1,0:T(8,128)(2,1)S(1)} %get-tuple-element.114), channel_id=1, source_target_pairs={{0,6},{1,7},{2,0},{3,1},{4,2},{5,3},{6,4},{7,5},{8,14},{9,15},{10,... | collective-permute-start | bytes 165896 | tf_op jit(solution)/shard_map/ppermute | solution.py:401
  102.8 10.1 %collective-permute-start.11 = (bf16[144,192]{1,0:T(8,128)(2,1)S(1)}, bf16[144,192]{1,0:T(8,128)(2,1)S(1)}, u32[]{:S(2)}, u32[]{:S(2)}) collective-permute-start(bf16[144,192]{1,0:T(8,128)(2,1)S(1)} %get-tuple-element.108), channel_id=1, source_target_pairs={{0,3},{1,2},{2,5},{3,4},{4,7},{5,6},{6,1},{7,0},{8,11},{9,10},{10,... | collective-permute-start | bytes 165896 | tf_op jit(solution)/shard_map/ppermute | solution.py:401
  105.4 7.5 %collective-permute-start.10 = (bf16[144,192]{1,0:T(8,128)(2,1)S(1)}, bf16[144,192]{1,0:T(8,128)(2,1)S(1)}, u32[]{:S(2)}, u32[]{:S(2)}) collective-permute-start(bf16[144,192]{1,0:T(8,128)(2,1)S(1)} %get-tuple-element.109), channel_id=1, source_target_pairs={{0,1},{1,0},{2,3},{3,2},{4,5},{5,4},{6,7},{7,6},{8,9},{9,8},{10,11... | collective-permute-start | bytes 165896 | tf_op jit(solution)/shard_map/ppermute | solution.py:401
  105.9 7.0 %collective-permute-start.9 = (bf16[144,192]{1,0:T(8,128)(2,1)S(1)}, bf16[144,192]{1,0:T(8,128)(2,1)S(1)}, u32[]{:S(2)}, u32[]{:S(2)}) collective-permute-start(bf16[144,192]{1,0:T(8,128)(2,1)S(1)} %get-tuple-element.110), channel_id=1, source_target_pairs={{0,2},{1,3},{2,4},{3,5},{4,6},{5,7},{6,0},{7,1},{8,10},{9,11},{10,... | collective-permute-start | bytes 165896 | tf_op jit(solution)/shard_map/ppermute | solution.py:401
  214.2 4.7 %copy-start.43 = (f32[2,192,192]{2,1,0:T(8,128)S(1)}, f32[2,192,192]{2,1,0:T(8,128)}, u32[]{:S(2)}) copy-start(f32[2,192,192]{2,1,0:T(8,128)} %get-tuple-element.97) | copy-start | bytes 884740
  214.2 4.7 %copy-start.44 = (f32[2,192,192]{2,1,0:T(8,128)S(1)}, f32[2,192,192]{2,1,0:T(8,128)}, u32[]{:S(2)}) copy-start(f32[2,192,192]{2,1,0:T(8,128)} %get-tuple-element.98) | copy-start | bytes 884740
  214.2 5.8 %copy-start.1 = (f32[1,2,4,2,6,3312]{5,3,4,2,1,0:T(2,128)S(1)}, f32[1,2,4,2,6,3312]{5,3,4,2,1,0:T(2,128)}, u32[]{:S(2)}) copy-start(f32[1,2,4,2,6,3312]{5,3,4,2,1,0:T(2,128)} %param.20) | copy-start | bytes 3815428
  (36 other events, 60.8 us)
